TPU v7x, 512 devices: a whole 4x4x16 slice. The times are simulated.
512 devices in a mesh: space: 128 (over z_lo, x, y), vec: 4 (over z_hi, core).
Axes of the slice: x: 4, y: 4, z: 16 (z_hi: 2, z_lo: 8; z = z_hi * 8 + z_lo), core: 2. Of those that a mesh axis runs over, the one named last changes fastest.
Arguments:
- vectors: bfloat16 [8, 32, 6, 128, 2048], P(None, 'vec', None, 'space'), may hold values from -3 to 3
- gauge_links: bfloat16 [3, 18, 128, 2048], P(None, None, 'space'), may hold values from -2.5 to 2.5
- momentum: int32 [3], replicated, may hold values from -2 to 2
- directions: int32 [2], replicated, may hold values from 0 to 2, as said below
- blocks: int32 [3], replicated, may hold values from 0 to 7, as said below
Outputs:
- elementals: float32 [2, 32, 1024], P(None, 'vec')
Inputs may be any that keep to these rules, and one draw needn't show every extreme that they name: `directions`: at least one of the 2 steps runs along the third dimension, and not all steps share one direction. Three different blocks, among them the first and the last stored block.
All inputs are finite; a program needn't handle non-finite values.
Results may differ from a plain program's by a relative error of at most 0.0075.
Values may be sent and summed in bfloat16 or wider, within the bound.
A program may use at most 64 MiB of HBM per device.

v0:
```python
import math

import jax
import jax.numpy as jnp
from jax import lax
from jax.sharding import PartitionSpec as P

DISP = 2
LX = 32
LY = 64


TWO_PI = 2.0 * math.pi


def shifted(value, axis, steps):
    count = lax.axis_size(axis)
    pairs = [(source, (source + steps) % count) for source in range(count)]
    return lax.ppermute(value, axis, pairs)


def link_apply(links_now, field):
    comps = []
    for c in range(3):
        real_part = 0.0
        imag_part = 0.0
        for b in range(3):
            link_real = links_now[(c * 3 + b) * 2].astype(jnp.float32)
            link_imag = links_now[(c * 3 + b) * 2 + 1].astype(jnp.float32)
            field_real = field[:, 2 * b].astype(jnp.float32)
            field_imag = field[:, 2 * b + 1].astype(jnp.float32)
            real_part = real_part + link_real * field_real - link_imag * field_imag
            imag_part = imag_part + link_real * field_imag + link_imag * field_real
        comps.append(real_part)
        comps.append(imag_part)
    return jnp.stack(comps, axis=1)


def roll_plane(field, first_axis):
    shape = field.shape
    grid = field.reshape(shape[:-1] + (LX, LY))
    if first_axis:
        moved = jnp.roll(grid, -1, axis=-2)
    else:
        moved = jnp.roll(grid, -1, axis=-1)
    return moved.reshape(shape)


def pick_neighbour(direction, field, upper):
    return jnp.where(
        direction == 0,
        roll_plane(field, True),
        jnp.where(direction == 1, roll_plane(field, False), upper),
    )


def apply_phase(field, cosines, sines):
    comps = []
    for a in range(3):
        field_real = field[:, 2 * a].astype(jnp.float32)
        field_imag = field[:, 2 * a + 1].astype(jnp.float32)
        comps.append(cosines * field_real + sines * field_imag)
        comps.append(cosines * field_imag - sines * field_real)
    return jnp.stack(comps, axis=1).astype(jnp.bfloat16)


def cross_table(left, right):
    parts = []
    for a in range(3):
        b = (a + 1) % 3
        c = (a + 2) % 3
        lbr = left[:, 2 * b].astype(jnp.float32)[:, None]
        lbi = left[:, 2 * b + 1].astype(jnp.float32)[:, None]
        lcr = left[:, 2 * c].astype(jnp.float32)[:, None]
        lci = left[:, 2 * c + 1].astype(jnp.float32)[:, None]
        rbr = right[:, 2 * b].astype(jnp.float32)[None]
        rbi = right[:, 2 * b + 1].astype(jnp.float32)[None]
        rcr = right[:, 2 * c].astype(jnp.float32)[None]
        rci = right[:, 2 * c + 1].astype(jnp.float32)[None]
        parts.append((lbr * rcr - lbi * rci - (lcr * rbr - lci * rbi)).astype(jnp.bfloat16))
        parts.append((lbr * rci + lbi * rcr - (lcr * rbi + lci * rbr)).astype(jnp.bfloat16))
    table = jnp.concatenate(parts, axis=-1)
    return table.reshape(left.shape[0] * right.shape[0], -1)


def contract_piece(qfield, left, right):
    table = cross_table(left, right)
    real_rows = []
    imag_rows = []
    for a in range(3):
        real_rows += [qfield[:, 2 * a], -qfield[:, 2 * a + 1]]
        imag_rows += [qfield[:, 2 * a + 1], qfield[:, 2 * a]]
    real_rows = jnp.concatenate(real_rows, axis=-1)
    imag_rows = jnp.concatenate(imag_rows, axis=-1)
    dims = (((1,), (1,)), ((), ()))
    real_out = lax.dot_general(real_rows, table, dims, preferred_element_type=jnp.float32)
    imag_out = lax.dot_general(imag_rows, table, dims, preferred_element_type=jnp.float32)
    return jnp.stack([real_out, imag_out])


def contract_blocks(qfield, left, right):
    sites = qfield.shape[-1]
    width = min(512, sites)
    count = sites // width
    start_total = jnp.zeros((2, qfield.shape[0], left.shape[0] * right.shape[0]), jnp.float32)

    def add_block(turn, total):
        return total + contract_piece(qfield, left, right)

    return lax.fori_loop(0, count, add_block, start_total)


def shards(vectors, gauge_links, momentum, directions, blocks):
    first = lax.dynamic_index_in_dim(vectors, blocks[0], 0, keepdims=False)
    second = lax.dynamic_index_in_dim(vectors, blocks[1], 0, keepdims=False)
    third = lax.dynamic_index_in_dim(vectors, blocks[2], 0, keepdims=False)
    own = first.shape[0]
    sites = first.shape[-1]
    planes = lax.axis_size("space")
    moved = first
    for s in range(DISP):
        d = directions[s]
        upper = shifted(moved, "space", -1)
        candidate = pick_neighbour(d, moved, upper)
        links_now = lax.dynamic_index_in_dim(gauge_links, d, 0, keepdims=False)
        moved = link_apply(links_now, candidate).astype(jnp.bfloat16)
    index = jnp.arange(LX * LY, dtype=jnp.int32)
    x_coord = index // LY
    y_coord = index % LY
    z_coord = lax.axis_index("space")
    fraction = (momentum[0] * x_coord % LX).astype(jnp.float32) / LX
    fraction = fraction + (momentum[1] * y_coord % LY).astype(jnp.float32) / LY
    fraction = fraction + (momentum[2] * z_coord % planes).astype(jnp.float32) / planes
    angles = (TWO_PI * fraction)[None, :]
    phased = apply_phase(moved, jnp.cos(angles), jnp.sin(angles)).reshape(own, 6, sites)
    second_flat = second.reshape(own, 6, sites)
    third_flat = third.reshape(own, 6, sites)
    every_phased, every_second, every_third = (
        lax.all_to_all(phased, "vec", split_axis=2, concat_axis=0, tiled=True),
        lax.all_to_all(second_flat, "vec", split_axis=2, concat_axis=0, tiled=True),
        lax.all_to_all(third_flat, "vec", split_axis=2, concat_axis=0, tiled=True),
    )
    partial_value = contract_blocks(every_phased, every_second, every_third)
    mine = lax.psum_scatter(partial_value, "vec", scatter_dimension=1, tiled=True)
    summed = lax.psum(mine, "space")
    return summed * (1.0 / math.sqrt(LX * LY * planes))


def solution(mesh):
    in_specs = (P(None, "vec", None, "space", None), P(None, None, "space", None), P(), P(), P())
    out_specs = P(None, "vec", None)
    return jax.shard_map(shards, mesh=mesh, in_specs=in_specs, out_specs=out_specs, check_vma=False)
```

profile of v0, /device:TPU:1, one launch (start us, length us, event | category | flops | bytes accessed | tf_op | source)
XLA Modules:
  0.0 2002.3 jit_solution(4484627519870315242)
XLA Ops:
  6.5 1.4 fusion.171
  13.5 1.2 constant_dynamic-slice_fusion.35
  14.7 4.0 copy.35
  18.6 3.7 bitcast_bitcast_fusion
  22.3 5.7 reshape.1686
  28.0 16.7 all-to-all-start.2
  44.7 10.0 collective-permute-start
  62.7 4.0 copy.32
  66.6 3.7 bitcast_bitcast_fusion.1
  70.3 5.6 reshape.1688
  78.4 1.3 fusion.157
  81.8 2.4 collective-permute-start.1
  85.3 4.6 collective-permute-done.1
  90.2 12.8 all-to-all-start.1
  103.1 4.0 copy.29
  107.0 5.7 reshape.1684
  112.7 4.8 reshape.1687
  117.5 4.3 copy.40
  121.8 12.0 all-to-all-start
  133.9 4.8 reshape.1689
  138.6 4.3 copy.39
  143.1 3.5 subtract_convert_fusion
  146.6 1.1 constant_dynamic-update-slice_fusion.29
  148.8 1.1 constant_dynamic-update-slice_fusion.27
  151.0 1.1 constant_dynamic-update-slice_fusion.25
  153.3 4.9 reshape.1685
  158.2 4.3 copy.38
  162.7 4.7 convolution_bitcast_fusion.1
  167.4 4.8 convolution_bitcast_fusion
  173.0 53.7 %reduce-scatter.2.cloned.1.call-done = f32[2,8,1024]{2,1,0:T(8,128)} async-done(((f32[2,32,1024]{2,1,0:T(8,128)}), f32[2,8,1024]{2,1,0:T(8,128)}) %reduce-scatter.2.cloned.1.call-update) | async-done | bytes 65552 | tf_op jit(solution)/shard_map/reduce_scatter | solution.py:144
  226.7 1767.3 %all-reduce.2.cloned.1.call-done = f32[2,8,1024]{2,1,0:T(8,128)} async-done(((f32[2,8,1024]{2,1,0:T(8,128)}), f32[2,8,1024]{2,1,0:T(8,128)}) %all-reduce.2.cloned.1.call-update) | async-done | bytes 65552 | tf_op jit(solution)/shard_map/psum | solution.py:145
  1994.0 1.5 broadcast_multiply_fusion
  (76 shorter events, 10.9 us)
Async XLA Ops:
  28.0 27.4 %copy-start.2 = (s32[2]{0:T(128)S(1)}, s32[2]{0:T(128)}, u32[]{:S(2)}) copy-start(s32[2]{0:T(128)} %param.8) | copy-start | bytes 28
  28.0 33.3 %copy-start.1 = (s32[3]{0:T(128)S(1)}, s32[3]{0:T(128)}, u32[]{:S(2)}) copy-start(s32[3]{0:T(128)} %param.7) | copy-start | bytes 40
  28.0 62.2 %all-to-all-start.2 = ((bf16[4,2,12288]{2,1,0:T(2,128)(2,1)}), bf16[4,2,12288]{2,1,0:T(2,128)(2,1)S(1)}, u32[]{:S(2)}, u32[]{:S(2)}) async-start(bf16[4,2,12288]{2,1,0:T(2,128)(2,1)} %reshape.1686), calls=%async_computation.2 | async-start | bytes 393216 | tf_op jit(solution)/shard_map/all_to_all | solution.py:141
  44.7 35.5 %collective-permute-start = (bf16[8,6,1,2048]{3,0,2,1:T(8,128)(2,1)S(1)}, bf16[8,6,1,2048]{3,0,2,1:T(8,128)(2,1)S(1)}, u32[]{:S(2)}, u32[]{:S(2)}) collective-permute-start(bf16[8,6,1,2048]{3,0,2,1:T(8,128)(2,1)S(1)} %bitcast.284), channel_id=1, source_target_pairs={{0,508},{4,0},{8,4},{12,8},{16,12},{20,16},{24,20},{28,24},{32,28}... | collective-permute-start | bytes 589832 | tf_op jit(solution)/shard_map/ppermute | solution.py:19
  76.0 3.7 copy-start
  81.8 8.1 collective-permute-start.1
  90.2 31.6 %all-to-all-start.1 = ((bf16[4,2,12288]{2,1,0:T(2,128)(2,1)}), bf16[4,2,12288]{2,1,0:T(2,128)(2,1)S(1)}, u32[]{:S(2)}, u32[]{:S(2)}) async-start(bf16[4,2,12288]{2,1,0:T(2,128)(2,1)} %reshape.1688), calls=%async_computation.1 | async-start | bytes 393216 | tf_op jit(solution)/shard_map/all_to_all | solution.py:140
  121.8 31.5 %all-to-all-start = ((bf16[4,2,12288]{2,1,0:T(2,128)(2,1)}), bf16[4,2,12288]{2,1,0:T(2,128)(2,1)S(1)}, u32[]{:S(2)}, u32[]{:S(2)}) async-start(bf16[4,2,12288]{2,1,0:T(2,128)(2,1)} %reshape.1684), calls=%async_computation | async-start | bytes 393216 | tf_op jit(solution)/shard_map/all_to_all | solution.py:139
  133.9 92.8 %reduce-scatter.2.cloned.1.call-start = ((), (), s32[]{:S(2)}) async-start(), calls=%async_computation.4 | async-start | bytes 327680 | tf_op jit(solution)/shard_map/reduce_scatter | solution.py:144
  172.9 1821.1 %all-reduce.2.cloned.1.call-start = ((), (), s32[]{:S(2)}) async-start(), calls=%async_computation.5 | async-start | bytes 131072 | tf_op jit(solution)/shard_map/psum | solution.py:145
Sparse Core Ops, SparseCore 0:
  173.1 53.5 reduce-scatter.1
  229.8 1764.1 all-reduce.1
where the time goes:
time: 2020 us; the launch traced here: 2000 us
  waiting for transfers between devices  1830 us (91%)
  local copies, waits for them, and re-layouts  77.6 us (4%)
  starting transfers between devices  53.9 us (3%)
  between operations  26.6 us (1%)
    psum x1, waiting for transfers between devices, shards(): summed = lax.psum(mine, 'space')  1770 us
    reduce_scatter x1, waiting for transfers between devices, shards(): lax.psum_scatter(partial_value, 'vec', scatter_dimension=1, tiled=True)  53.7 us
    unnamed x29, local copies, waits for them, and re-layouts  44.5 us
  transfers between devices with their start and end apart: 7, of which 3 were waited for; matrix products, arithmetic and copies ran while one was open for 3% of the time, Pallas kernels for 0%

commit v1 on v0

v1 whole, which is shorter than its diff:
```python
import functools
import math

import jax
import jax.numpy as jnp
from jax import lax
from jax.experimental import pallas as pl
from jax.experimental.pallas import tpu as pltpu
from jax.sharding import PartitionSpec as P

LX = 32
LY = 64
SITES = LX * LY
PLANES = 128
TWO_PI = 2.0 * math.pi
MESH = pl.DeviceIdType.MESH
F32 = jnp.float32
BF16 = jnp.bfloat16
LANES = 128
QUARTER = SITES // 4
CHUNKS = QUARTER // LANES


def link_rows(links, field):
    out = []
    for c in range(3):
        real_part = None
        for b in range(3):
            at = (c * 3 + b) * 2
            lr = links[at : at + 1]
            li = links[at + 1 : at + 2]
            fr = field[16 * b : 16 * b + 8]
            fi = field[16 * b + 8 : 16 * b + 16]
            re = lr * fr - li * fi
            im = lr * fi + li * fr
            real_part, imag_part = (re, im) if real_part is None else (real_part + re, imag_part + im)
        out += [real_part, imag_part]
    return out


def rolled(direction, row):
    lane = lax.broadcasted_iota(jnp.int32, row.shape, 1)
    next_x = pltpu.roll(row, SITES - LY, 1)
    next_y = jnp.where(
        lax.rem(lane, LY) == LY - 1, pltpu.roll(row, LY - 1, 1), pltpu.roll(row, SITES - 1, 1)
    )
    return jnp.where(direction == 0, next_x, next_y)


def kernel(
    momentum, directions, blocks, vec_hbm, links_hbm, out,
    vec_v, links_v, st_send, st_recv, st_wide, roll_v, shift_send, shift_recv, cos_v, sin_v,
    phi_send, phi_recv, table, e_send, e_recv, z_send, z_recv, ag_recv,
    load_sem, own_sem, shift_sems, st_sems, phi_send_sem, phi_recv_sems, e_sems, z_sems, ag_sems,
):
    space = lax.axis_index("space")
    vec = lax.axis_index("vec")
    flat = lax.rem(space, 16)
    zlow = lax.div(space, 16)
    half = lax.div(vec, 2)
    core = lax.rem(vec, 2)
    zee = half * 8 + zlow

    def flat_peer(d):
        return zlow * 16 + lax.rem(flat + lax.rem(d, 16), 16), half * 2 + lax.rem(core + lax.div(d, 16), 2)

    def z_peer(d):
        z = lax.rem(zee + d, 16)
        return lax.rem(z, 8) * 16 + flat, lax.div(z, 8) * 2 + core

    def vec_peer(d):
        return space, lax.rem(vec + d, 4)

    below = (lax.rem(space + PLANES - 1, PLANES), vec)
    above = (lax.rem(space + 1, PLANES), vec)
    cross_core = (space, (1 - half) * 2 + (1 - core))

    load_vec = pltpu.make_async_copy(vec_hbm, vec_v, load_sem.at[0])
    load_links = pltpu.make_async_copy(links_hbm, links_v, load_sem.at[1])
    load_vec.start()
    load_links.start()

    barrier = pltpu.get_barrier_semaphore()

    def greet(device):
        pl.semaphore_signal(barrier, inc=1, device_id=device, device_id_type=MESH)

    greet(cross_core)

    @pl.loop(1, 16)
    def _(d):
        greet(z_peer(d))

    greet(below)
    greet(above)

    @pl.loop(1, 32)
    def _(d):
        greet(flat_peer(d))

    first_step = directions[0]
    z_first = first_step == 2
    inplane = jnp.where(z_first, directions[1], first_step)

    load_vec.wait()
    load_links.wait()
    for q in range(4):
        at = slice(q * QUARTER, (q + 1) * QUARTER)
        st_send[q, 0:48] = vec_v[blocks[1], :, at]
        st_send[q, 48:96] = vec_v[blocks[2], :, at]

    for b in range(6):
        row = vec_v[blocks[0], (b // 2) * 16 : (b // 2) * 16 + 16, :].astype(F32)
        row = row[(b % 2) * 8 : (b % 2) * 8 + 8]
        roll_v[b * 8 : b * 8 + 8] = rolled(inplane, row)

    @pl.loop(0, SITES // 256)
    def _(t):
        at = pl.ds(t * 256, 256)
        links = links_v[inplane, :, at].astype(F32)
        moved = jnp.concatenate(link_rows(links, roll_v[:, at]), axis=0).astype(BF16)
        shift_send[:, at] = jnp.where(z_first, vec_v[blocks[0], :, at], moved)

    site = lax.broadcasted_iota(jnp.int32, (8, SITES), 1)
    fraction = ((momentum[0] * lax.div(site, LY)) & (LX - 1)).astype(F32) / LX
    fraction = fraction + ((momentum[1] * lax.rem(site, LY)) & (LY - 1)).astype(F32) / LY
    fraction = fraction + ((momentum[2] * space) & (PLANES - 1)).astype(F32) / PLANES
    angles = TWO_PI * fraction
    cos_v[...] = jnp.cos(angles)
    sin_v[...] = jnp.sin(angles)

    pl.semaphore_wait(barrier, 15 + 31 + 3)

    shift = pltpu.make_async_remote_copy(
        src_ref=shift_send, dst_ref=shift_recv, send_sem=shift_sems.at[0], recv_sem=shift_sems.at[1],
        device_id=below, device_id_type=MESH,
    )
    shift.start()
    for d in (2, 1, 3):
        target = lax.rem(vec + d, 4)
        pltpu.make_async_remote_copy(
            src_ref=st_send.at[target], dst_ref=st_recv.at[vec], send_sem=st_sems.at[0],
            recv_sem=st_sems.at[1], device_id=vec_peer(d), device_id_type=MESH,
        ).start()
    own_st = pltpu.make_async_copy(st_send.at[vec], st_recv.at[vec], own_sem.at[0])
    own_st.start()

    shift.wait_recv()

    @pl.loop(0, SITES // 256)
    def _(t):
        at = pl.ds(t * 256, 256)
        links = links_v[2, :, at].astype(F32)
        moved = jnp.concatenate(link_rows(links, shift_recv[:, at].astype(F32)), axis=0)
        shift_recv[:, at] = moved.astype(BF16)

    for b in range(6):
        row = shift_recv[(b // 2) * 16 : (b // 2) * 16 + 16, :].astype(F32)
        row = row[(b % 2) * 8 : (b % 2) * 8 + 8]
        roll_v[b * 8 : b * 8 + 8] = rolled(inplane, row)

    @pl.loop(0, SITES // LANES)
    def _(t):
        at = pl.ds(t * LANES, LANES)
        links = links_v[inplane, :, at].astype(F32)
        moved = jnp.concatenate(link_rows(links, roll_v[:, at]), axis=0).astype(BF16)
        moved = jnp.where(z_first, moved, shift_recv[:, at]).astype(F32)
        cosines = cos_v[:, at]
        sines = sin_v[:, at]
        rows = []
        for a in range(3):
            re = moved[16 * a : 16 * a + 8]
            im = moved[16 * a + 8 : 16 * a + 16]
            rows += [cosines * re + sines * im, cosines * im - sines * re]
        phi_send[lax.rem(t, CHUNKS), lax.div(t, CHUNKS)] = jnp.concatenate(rows, axis=0).astype(BF16)

    st_three = st_recv.at[pl.ds(0, 3)]
    pltpu.make_async_copy(st_three, st_three, st_sems.at[0]).wait()
    for n in range(CHUNKS):
        for d in (2, 1, 3):
            target = lax.rem(vec + d, 4)
            pltpu.make_async_remote_copy(
                src_ref=phi_send.at[n, target], dst_ref=phi_recv.at[n, vec], send_sem=phi_send_sem.at[0],
                recv_sem=phi_recv_sems.at[n], device_id=vec_peer(d), device_id_type=MESH,
            ).start()
    own_phi = []
    for n in range(CHUNKS):
        own_phi.append(pltpu.make_async_copy(phi_send.at[n, vec], phi_recv.at[n, vec], own_sem.at[1 + n]))
        own_phi[-1].start()

    own_st.wait()
    pltpu.make_async_copy(st_three, st_three, st_sems.at[1]).wait()

    @pl.loop(0, 4)
    def _(source):
        st_wide[source] = st_recv[source].astype(F32)

    @pl.loop(0, CHUNKS * 4)
    def _(turn):
        n = lax.div(turn, 4)
        source = lax.rem(turn, 4)
        at = pl.ds(n * LANES, LANES)
        right = [[st_wide[k, 48 + 8 * b : 56 + 8 * b, at] for b in range(6)] for k in range(4)]
        for j in range(8):
            left = [
                jnp.broadcast_to(st_wide[source, 8 * b + j : 8 * b + j + 1, at], (8, LANES)) for b in range(6)
            ]
            start = source * 256 + j * 32
            for a in range(3):
                b = 2 * ((a + 1) % 3)
                c = 2 * ((a + 2) % 3)
                reals = []
                imags = []
                for k in range(4):
                    rbr, rbi, rcr, rci = right[k][b], right[k][b + 1], right[k][c], right[k][c + 1]
                    lbr, lbi, lcr, lci = left[b], left[b + 1], left[c], left[c + 1]
                    reals.append(lbr * rcr - lbi * rci - (lcr * rbr - lci * rbi))
                    imags.append(lbr * rci + lbi * rcr - (lcr * rbi + lci * rbr))
                table[n, pl.ds(start, 32), 2 * a * LANES : (2 * a + 1) * LANES] = jnp.concatenate(
                    reals, axis=0
                ).astype(BF16)
                table[n, pl.ds(start, 32), (2 * a + 1) * LANES : (2 * a + 2) * LANES] = jnp.concatenate(
                    imags, axis=0
                ).astype(BF16)

    total = None
    for n in range(CHUNKS):
        own_phi[n].wait()
        phi_three = phi_recv.at[n, pl.ds(0, 3)]
        pltpu.make_async_copy(phi_three, phi_three, phi_recv_sems.at[n]).wait()
        real_rows = []
        imag_rows = []
        for source in range(4):
            field = phi_recv[n, source].astype(F32)
            reals = [field[16 * a : 16 * a + 8] for a in range(3)]
            imags = [field[16 * a + 8 : 16 * a + 16] for a in range(3)]
            real_rows.append(jnp.concatenate([x for a in range(3) for x in (reals[a], -imags[a])], axis=1))
            imag_rows.append(jnp.concatenate([x for a in range(3) for x in (imags[a], reals[a])], axis=1))
        rows = jnp.concatenate(real_rows + imag_rows, axis=0).astype(BF16)
        term = lax.dot_general(rows, table[n], (((1,), (1,)), ((), ())), preferred_element_type=F32)
        total = term if total is None else total + term
    for part in range(2):
        for h in range(2):
            for c in range(2):
                at = part * 32 + (2 * h + c) * 8
                for tile in range(8):
                    e_send[c, part * 8 + tile, h] = total[at : at + 8, tile * LANES : (tile + 1) * LANES]

    @pl.loop(1, 32)
    def _(d):
        to_space, to_vec = flat_peer(d)
        pltpu.make_async_remote_copy(
            src_ref=e_send.at[lax.rem(to_vec, 2), lax.rem(to_space, 16)], dst_ref=e_recv.at[d - 1],
            send_sem=e_sems.at[0], recv_sem=e_sems.at[1], device_id=(to_space, to_vec), device_id_type=MESH,
        ).start()

    plane_sum = e_send[core, flat]
    pltpu.make_async_copy(e_recv, e_recv, e_sems.at[1]).wait()
    for d in range(31):
        plane_sum = plane_sum + e_recv[d]
    z_send[...] = plane_sum

    @pl.loop(1, 16)
    def _(d):
        to_space, to_vec = z_peer(d)
        pltpu.make_async_remote_copy(
            src_ref=z_send.at[lax.div(to_vec, 2)], dst_ref=z_recv.at[zee], send_sem=z_sems.at[0],
            recv_sem=z_sems.at[1], device_id=(to_space, to_vec), device_id_type=MESH,
        ).start()

    z_recv[zee] = z_send[half]
    z_others = z_recv.at[pl.ds(0, 15)]
    pltpu.make_async_copy(z_others, z_others, z_sems.at[1]).wait()
    whole = z_recv[0]
    for z in range(1, 16):
        whole = whole + z_recv[z]
    ag_recv[flat] = whole * (1.0 / math.sqrt(SITES * PLANES))

    @pl.loop(1, 16)
    def _(d):
        pltpu.make_async_remote_copy(
            src_ref=ag_recv.at[flat], dst_ref=ag_recv.at[flat], send_sem=ag_sems.at[0],
            recv_sem=ag_sems.at[1], device_id=flat_peer(d), device_id_type=MESH,
        ).start()

    ag_others = ag_recv.at[pl.ds(0, 15)]
    pltpu.make_async_copy(ag_others, ag_others, ag_sems.at[1]).wait()
    for part in range(2):
        for tile in range(8):
            out[part, :, tile * LANES : (tile + 1) * LANES] = ag_recv[part * 8 + tile]

    shift.wait_send()
    phi_three = phi_recv.at[:, pl.ds(0, 3)]
    pltpu.make_async_copy(phi_three, phi_three, phi_send_sem.at[0]).wait()
    pltpu.make_async_copy(e_recv, e_recv, e_sems.at[0]).wait()
    pltpu.make_async_copy(z_others, z_others, z_sems.at[0]).wait()
    pltpu.make_async_copy(ag_others, ag_others, ag_sems.at[0]).wait()


def shards(vectors, gauge_links, momentum, directions, blocks):
    nblk = vectors.shape[0]
    vec = vectors.transpose(0, 2, 3, 1, 4).reshape(nblk, 48, SITES)
    links = gauge_links.reshape(3, 18, SITES)
    smem = pl.BlockSpec(memory_space=pltpu.SMEM)
    return pl.pallas_call(
        kernel,
        name="elementals",
        out_shape=jax.ShapeDtypeStruct((2, 8, 1024), F32),
        in_specs=[smem, smem, smem, pl.BlockSpec(memory_space=pl.ANY), pl.BlockSpec(memory_space=pl.ANY)],
        out_specs=pl.BlockSpec(memory_space=pltpu.VMEM),
        scratch_shapes=[
            pltpu.VMEM((nblk, 48, SITES), BF16),
            pltpu.VMEM((3, 18, SITES), BF16),
            pltpu.VMEM((4, 96, QUARTER), BF16),
            pltpu.VMEM((4, 96, QUARTER), BF16),
            pltpu.VMEM((4, 96, QUARTER), F32),
            pltpu.VMEM((48, SITES), F32),
            pltpu.VMEM((48, SITES), BF16),
            pltpu.VMEM((48, SITES), BF16),
            pltpu.VMEM((8, SITES), F32),
            pltpu.VMEM((8, SITES), F32),
            pltpu.VMEM((CHUNKS, 4, 48, LANES), BF16),
            pltpu.VMEM((CHUNKS, 4, 48, LANES), BF16),
            pltpu.VMEM((CHUNKS, 1024, 6 * LANES), BF16),
            pltpu.VMEM((2, 16, 2, 8, LANES), F32),
            pltpu.VMEM((31, 2, 8, LANES), F32),
            pltpu.VMEM((2, 8, LANES), F32),
            pltpu.VMEM((16, 8, LANES), F32),
            pltpu.VMEM((16, 8, LANES), F32),
            pltpu.SemaphoreType.DMA((2,)),
            pltpu.SemaphoreType.DMA((1 + CHUNKS,)),
            pltpu.SemaphoreType.DMA((2,)),
            pltpu.SemaphoreType.DMA((2,)),
            pltpu.SemaphoreType.DMA((1,)),
            pltpu.SemaphoreType.DMA((CHUNKS,)),
            pltpu.SemaphoreType.DMA((2,)),
            pltpu.SemaphoreType.DMA((2,)),
            pltpu.SemaphoreType.DMA((2,)),
        ],
        compiler_params=pltpu.CompilerParams(
            collective_id=1, has_side_effects=True, vmem_limit_bytes=40 * 2**20
        ),
    )(momentum, directions, blocks, vec, links)


def solution(mesh):
    in_specs = (P(None, "vec", None, "space", None), P(None, None, "space", None), P(), P(), P())
    out_specs = P(None, "vec", None)
    return jax.shard_map(shards, mesh=mesh, in_specs=in_specs, out_specs=out_specs, check_vma=False)
```

time: 2020 us -> 80.3 us (0.04)
  waiting for transfers between devices: 1830 us -> 0 us
  Pallas kernels: 0 us -> 75.2 us
  local copies, waits for them, and re-layouts: 77.6 us -> 4.96 us
  starting transfers between devices: 53.9 us -> 0 us
  between operations: 26.6 us -> 0.01 us
    psum x1 -> x0, waiting for transfers between devices: 1770 us -> none  [shards(): summed = lax.psum(mine, 'space')]
    pallas_call x0 -> x1, Pallas kernels: none -> 75.2 us  [shards(): pl.pallas_call(kernel, name='elementals', out_shape=jax.ShapeDtypeStruct(...]
    reduce_scatter x1 -> x0, waiting for transfers between devices: 53.7 us -> none  [shards(): lax.psum_scatter(partial_value, 'vec', scatter_dimension=1, tiled=True)]
    all_to_all x3 -> x0, starting transfers between devices: 41.5 us -> none  [the longest x1 16.7 us: shards(): lax.all_to_all(third_flat, 'vec', split_axis=2, concat_axis=0, tiled=True)]
    unnamed x29 -> x11, local copies, waits for them, and re-layouts: 44.5 us -> 4.96 us
  transfers between devices with their start and end apart: 7 -> 0, of which waited for: 3 -> 0; matrix products, arithmetic and copies ran while one was open for 3% -> 0% of each run, Pallas kernels for 0% -> 0%
where the time goes in v1:
time: 80.3 us; the launch traced here: 80.1 us
  Pallas kernels  75.2 us (94%)
  local copies, waits for them, and re-layouts  4.96 us (6%)
    pallas_call x1, Pallas kernels, shards(): pl.pallas_call(kernel, name='elementals', out_shape=jax.ShapeDtypeStruct(...  75.2 us
    unnamed x11, local copies, waits for them, and re-layouts  4.96 us

profile of v1, /device:TPU:1, one launch (start us, length us, event | category | flops | bytes accessed | tf_op | source)
XLA Modules:
  0.0 80.1 jit_solution(17133492101646913475)
XLA Ops:
  0.0 0.0 copy-start
  0.0 1.4 %copy-done = bf16[8,8,6,1,2048]{4,1,3,2,0:T(8,128)(2,1)S(1)} copy-done((bf16[8,8,6,1,2048]{4,1,3,2,0:T(8,128)(2,1)S(1)}, bf16[8,8,6,1,2048]{4,1,3,2,0:T(8,128)(2,1)}, u32[]{:S(2)}) %copy-start) | copy-done | bytes 1572888
  1.4 0.0 copy-start.1
  1.4 1.0 %copy-done.1 = bf16[3,18,1,2048]{3,1,2,0:T(8,128)(2,1)S(1)} copy-done((bf16[3,18,1,2048]{3,1,2,0:T(8,128)(2,1)S(1)}, bf16[3,18,1,2048]{3,1,2,0:T(8,128)(2,1)}, u32[]{:S(2)}) %copy-start.1) | copy-done | bytes 221208
  2.4 0.0 copy-start.2
  2.4 0.7 copy-done.2
  3.0 0.0 copy-start.3
  3.0 0.7 copy-done.3
  3.7 0.0 copy-start.4
  3.7 0.7 copy-done.4
  4.3 75.2 %elementals.1 = f32[2,8,1024]{2,1,0:T(8,128)S(1)} custom-call(s32[3]{0:T(128)S(1)} %copy-done.2, s32[2]{0:T(128)S(1)} %copy-done.3, s32[3]{0:T(128)S(1)} %copy-done.4, bf16[8,48,2048]{2,1,0:T(8,128)(2,1)S(1)} %bitcast.4, bf16[3,18,2048]{2,1,0:T(8,128)(2,1)S(1)} %bitcast.5), custom_call_target="tpu_custom_call" | custom-call | tf_op jit(solution)/shard_map/elementals/pallas_call | solution.py:305
  79.5 0.6 copy.7
Async XLA Ops:
  0.0 1.4 %copy-start = (bf16[8,8,6,1,2048]{4,1,3,2,0:T(8,128)(2,1)S(1)}, bf16[8,8,6,1,2048]{4,1,3,2,0:T(8,128)(2,1)}, u32[]{:S(2)}) copy-start(bf16[8,8,6,1,2048]{4,1,3,2,0:T(8,128)(2,1)} %param.5) | copy-start | bytes 4718596
  1.4 1.0 %copy-start.1 = (bf16[3,18,1,2048]{3,1,2,0:T(8,128)(2,1)S(1)}, bf16[3,18,1,2048]{3,1,2,0:T(8,128)(2,1)}, u32[]{:S(2)}) copy-start(bf16[3,18,1,2048]{3,1,2,0:T(8,128)(2,1)} %param.6) | copy-start | bytes 663556
  2.4 0.7 copy-start.2
  3.0 0.7 copy-start.3
  3.7 0.7 copy-start.4

commit v2 on v1

v2 whole, which is shorter than its diff:
```python
import functools
import math

import jax
import jax.numpy as jnp
from jax import lax
from jax.experimental import pallas as pl
from jax.experimental.pallas import tpu as pltpu
from jax.sharding import PartitionSpec as P

LX = 32
LY = 64
SITES = LX * LY
PLANES = 128
TWO_PI = 2.0 * math.pi
MESH = pl.DeviceIdType.MESH
F32 = jnp.float32
BF16 = jnp.bfloat16
LANES = 128
QUARTER = SITES // 4
CHUNKS = QUARTER // LANES
FLAT_ORDER = sorted(range(1, 32), key=lambda d: -(min(d // 4 % 4, 4 - d // 4 % 4) + min(d % 4, 4 - d % 4)))


def link_rows(links, field):
    out = []
    for c in range(3):
        real_part = None
        for b in range(3):
            at = (c * 3 + b) * 2
            lr = links[at : at + 1]
            li = links[at + 1 : at + 2]
            fr = field[16 * b : 16 * b + 8]
            fi = field[16 * b + 8 : 16 * b + 16]
            re = lr * fr - li * fi
            im = lr * fi + li * fr
            real_part, imag_part = (re, im) if real_part is None else (real_part + re, imag_part + im)
        out += [real_part, imag_part]
    return out


def rolled(direction, row):
    lane = lax.broadcasted_iota(jnp.int32, row.shape, 1)
    next_x = pltpu.roll(row, SITES - LY, 1)
    next_y = jnp.where(
        lax.rem(lane, LY) == LY - 1, pltpu.roll(row, LY - 1, 1), pltpu.roll(row, SITES - 1, 1)
    )
    return jnp.where(direction == 0, next_x, next_y)


def kernel(
    momentum_hbm, directions_hbm, blocks_hbm, vec_hbm, links_hbm, out,
    momentum, directions, blocks, vec_v, links_v, st_send, st_recv, st_wide, roll_v, shift_send, shift_recv, cos_v, sin_v,
    phi_send, phi_recv, table, e_send, e_recv, z_send, z_recv, ag_recv,
    load_sem, own_sem, shift_sems, st_sems, phi_send_sem, phi_recv_sems, e_sems, z_sems, ag_sems, known_sems,
):
    space = lax.axis_index("space")
    vec = lax.axis_index("vec")
    flat = lax.rem(space, 16)
    zlow = lax.div(space, 16)
    half = lax.div(vec, 2)
    core = lax.rem(vec, 2)
    zee = half * 8 + zlow

    def flat_peer(d):
        x = lax.rem(lax.div(flat, 4) + lax.rem(lax.div(d, 4), 4), 4)
        y = lax.rem(flat + lax.rem(d, 4), 4)
        return zlow * 16 + x * 4 + y, half * 2 + lax.rem(core + lax.div(d, 16), 2)

    def z_peer(d):
        z = lax.rem(zee + d, 16)
        return lax.rem(z, 8) * 16 + flat, lax.div(z, 8) * 2 + core

    def vec_peer(d):
        return space, lax.rem(vec + d, 4)

    below = (lax.rem(space + PLANES - 1, PLANES), vec)
    above = (lax.rem(space + 1, PLANES), vec)
    near = half * 2 + (1 - core)
    cross_core = (space, (1 - half) * 2 + (1 - core))

    barrier = pltpu.get_barrier_semaphore()

    def greet(device):
        pl.semaphore_signal(barrier, inc=1, device_id=device, device_id_type=MESH)

    greet(z_peer(8))
    greet(cross_core)
    greet(z_peer(1))
    greet(z_peer(15))
    greet(below)
    greet(above)

    @pl.loop(1, 32)
    def _(d):
        greet(flat_peer(d))

    loads = [
        pltpu.make_async_copy(source, target, load_sem.at[at])
        for at, (source, target) in enumerate(
            (
                (blocks_hbm, blocks), (vec_hbm, vec_v), (links_hbm, links_v),
                (directions_hbm, directions), (momentum_hbm, momentum),
            )
        )
    ]
    for load in loads:
        load.start()
    for load in loads:
        load.wait()

    def pass_on(at, steps):
        for d in (steps, 16 - steps):
            pl.semaphore_signal(known_sems.at[at], inc=1, device_id=z_peer(d), device_id_type=MESH)

    first_step = directions[0]
    z_first = first_step == 2
    inplane = jnp.where(z_first, directions[1], first_step)

    for q in range(4):
        at = slice(q * QUARTER, (q + 1) * QUARTER)
        st_send[q, 0:48] = vec_v[blocks[1], :, at]
        st_send[q, 48:96] = vec_v[blocks[2], :, at]

    pl.semaphore_wait(barrier, 31 + 6)

    for d in (2, 1, 3):
        target = lax.rem(vec + d, 4)
        pltpu.make_async_remote_copy(
            src_ref=st_send.at[target], dst_ref=st_recv.at[vec], send_sem=st_sems.at[0],
            recv_sem=st_sems.at[1], device_id=vec_peer(d), device_id_type=MESH,
        ).start()
    pass_on(0, 1)
    own_st = pltpu.make_async_copy(st_send.at[vec], st_recv.at[vec], own_sem.at[0])
    own_st.start()

    for b in range(6):
        row = vec_v[blocks[0], (b // 2) * 16 : (b // 2) * 16 + 16, :].astype(F32)
        row = row[(b % 2) * 8 : (b % 2) * 8 + 8]
        roll_v[b * 8 : b * 8 + 8] = rolled(inplane, row)

    @pl.loop(0, SITES // 256)
    def _(t):
        at = pl.ds(t * 256, 256)
        links = links_v[inplane, :, at].astype(F32)
        moved = jnp.concatenate(link_rows(links, roll_v[:, at]), axis=0).astype(BF16)
        shift_send[:, at] = jnp.where(z_first, vec_v[blocks[0], :, at], moved)

    shift = pltpu.make_async_remote_copy(
        src_ref=shift_send, dst_ref=shift_recv, send_sem=shift_sems.at[0], recv_sem=shift_sems.at[1],
        device_id=below, device_id_type=MESH,
    )
    shift.start()
    pl.semaphore_wait(known_sems.at[0], 2)
    pass_on(1, 2)
    site = lax.broadcasted_iota(jnp.int32, (8, SITES), 1)
    fraction = ((momentum[0] * lax.div(site, LY)) & (LX - 1)).astype(F32) / LX
    fraction = fraction + ((momentum[1] * lax.rem(site, LY)) & (LY - 1)).astype(F32) / LY
    fraction = fraction + ((momentum[2] * space) & (PLANES - 1)).astype(F32) / PLANES
    angles = TWO_PI * fraction
    cos_v[...] = jnp.cos(angles)
    sin_v[...] = jnp.sin(angles)

    shift.wait_recv()
    pl.semaphore_wait(known_sems.at[1], 2)
    pass_on(2, 4)

    @pl.loop(0, SITES // 256)
    def _(t):
        at = pl.ds(t * 256, 256)
        links = links_v[2, :, at].astype(F32)
        moved = jnp.concatenate(link_rows(links, shift_recv[:, at].astype(F32)), axis=0)
        shift_recv[:, at] = moved.astype(BF16)

    for b in range(6):
        row = shift_recv[(b // 2) * 16 : (b // 2) * 16 + 16, :].astype(F32)
        row = row[(b % 2) * 8 : (b % 2) * 8 + 8]
        roll_v[b * 8 : b * 8 + 8] = rolled(inplane, row)

    @pl.loop(0, SITES // LANES)
    def _(t):
        at = pl.ds(t * LANES, LANES)
        links = links_v[inplane, :, at].astype(F32)
        moved = jnp.concatenate(link_rows(links, roll_v[:, at]), axis=0).astype(BF16)
        moved = jnp.where(z_first, moved, shift_recv[:, at]).astype(F32)
        cosines = cos_v[:, at]
        sines = sin_v[:, at]
        rows = []
        for a in range(3):
            re = moved[16 * a : 16 * a + 8]
            im = moved[16 * a + 8 : 16 * a + 16]
            rows += [cosines * re + sines * im, cosines * im - sines * re]
        phi_send[lax.rem(t, CHUNKS), lax.div(t, CHUNKS)] = jnp.concatenate(rows, axis=0).astype(BF16)

    for n in range(CHUNKS):
        for d, sem in ((2, phi_recv_sems.at[n]), (None, phi_recv_sems.at[n]), (1, phi_recv_sems.at[CHUNKS])):
            to_vec = near if d == 1 else (lax.rem(vec + 2, 4) if d == 2 else cross_core[1])
            pltpu.make_async_remote_copy(
                src_ref=phi_send.at[n, to_vec], dst_ref=phi_recv.at[n, vec], send_sem=phi_send_sem.at[0],
                recv_sem=sem, device_id=(space, to_vec), device_id_type=MESH,
            ).start()
    own_phi = pltpu.make_async_copy(phi_send.at[:, vec], phi_recv.at[:, vec], own_sem.at[1])
    own_phi.start()

    pl.semaphore_wait(known_sems.at[2], 2)
    st_three = st_recv.at[pl.ds(0, 3)]
    own_st.wait()
    pltpu.make_async_copy(st_three, st_three, st_sems.at[1]).wait()

    @pl.loop(0, 4)
    def _(source):
        st_wide[source] = st_recv[source].astype(F32)

    @pl.loop(0, CHUNKS * 4)
    def _(turn):
        n = lax.div(turn, 4)
        source = lax.rem(turn, 4)
        at = pl.ds(n * LANES, LANES)
        right = [[st_wide[k, 48 + 8 * b : 56 + 8 * b, at] for b in range(6)] for k in range(4)]
        for j in range(8):
            left = [
                jnp.broadcast_to(st_wide[source, 8 * b + j : 8 * b + j + 1, at], (8, LANES)) for b in range(6)
            ]
            start = source * 256 + j * 32
            for a in range(3):
                b = 2 * ((a + 1) % 3)
                c = 2 * ((a + 2) % 3)
                reals = []
                imags = []
                for k in range(4):
                    rbr, rbi, rcr, rci = right[k][b], right[k][b + 1], right[k][c], right[k][c + 1]
                    lbr, lbi, lcr, lci = left[b], left[b + 1], left[c], left[c + 1]
                    reals.append(lbr * rcr - lbi * rci - (lcr * rbr - lci * rbi))
                    imags.append(lbr * rci + lbi * rcr - (lcr * rbi + lci * rbr))
                table[n, pl.ds(start, 32), 2 * a * LANES : (2 * a + 1) * LANES] = jnp.concatenate(
                    reals, axis=0
                ).astype(BF16)
                table[n, pl.ds(start, 32), (2 * a + 1) * LANES : (2 * a + 2) * LANES] = jnp.concatenate(
                    imags, axis=0
                ).astype(BF16)

    def product(n, whose):
        real_rows = []
        imag_rows = []
        for c in range(2):
            field = phi_recv[n, 2 * whose + c].astype(F32)
            reals = [field[16 * a : 16 * a + 8] for a in range(3)]
            imags = [field[16 * a + 8 : 16 * a + 16] for a in range(3)]
            real_rows.append(jnp.concatenate([x for a in range(3) for x in (reals[a], -imags[a])], axis=1))
            imag_rows.append(jnp.concatenate([x for a in range(3) for x in (imags[a], reals[a])], axis=1))
        rows = jnp.concatenate(real_rows + imag_rows, axis=0).astype(BF16)
        return lax.dot_general(rows, table[n], (((1,), (1,)), ((), ())), preferred_element_type=F32)

    def scatter(at, total):
        for part in range(2):
            for c in range(2):
                start = part * 16 + c * 8
                for tile in range(8):
                    e_send[at, c, part * 8 + tile] = total[start : start + 8, tile * LANES : (tile + 1) * LANES]
        for d in FLAT_ORDER:
            to_space, to_vec = flat_peer(d)
            pltpu.make_async_remote_copy(
                src_ref=e_send.at[at, lax.rem(to_vec, 2), lax.rem(to_space, 16)], dst_ref=e_recv.at[at, d - 1],
                send_sem=e_sems.at[2], recv_sem=e_sems.at[at], device_id=(to_space, to_vec), device_id_type=MESH,
            ).start()

    def gathered(at):
        pltpu.make_async_copy(e_recv.at[at], e_recv.at[at], e_sems.at[at]).wait()
        total = e_send[at, core, flat]
        for d in range(31):
            total = total + e_recv[at, d]
        return total

    def send_z(at, d):
        to_space, to_vec = z_peer(d)
        pltpu.make_async_remote_copy(
            src_ref=z_send.at[at], dst_ref=z_recv.at[zee], send_sem=z_sems.at[2],
            recv_sem=z_sems.at[at], device_id=(to_space, to_vec), device_id_type=MESH,
        ).start()

    own_phi.wait()
    phi_near = phi_recv.at[:, 0]
    pltpu.make_async_copy(phi_near, phi_near, phi_recv_sems.at[CHUNKS]).wait()
    total = product(0, half)
    for n in range(1, CHUNKS):
        total = total + product(n, half)
    scatter(0, total)

    total = None
    for n in range(CHUNKS):
        phi_two = phi_recv.at[n, pl.ds(0, 2)]
        pltpu.make_async_copy(phi_two, phi_two, phi_recv_sems.at[n]).wait()
        term = product(n, 1 - half)
        total = term if total is None else total + term
    scatter(1, total)

    z_send[0] = gathered(0)
    z_recv[zee] = z_send[0]
    for step in range(1, 8):
        send_z(0, half * 8 + lax.rem(zlow + step, 8) - zee + 16)

    z_send[1] = gathered(1)
    for step in (0, 1, 7, 2, 6, 3, 5, 4):
        send_z(1, (1 - half) * 8 + lax.rem(zlow + step, 8) - zee + 16)

    z_same = z_recv.at[pl.ds(0, 7)]
    z_other = z_recv.at[pl.ds(0, 8)]
    pltpu.make_async_copy(z_same, z_same, z_sems.at[0]).wait()
    pltpu.make_async_copy(z_other, z_other, z_sems.at[1]).wait()
    whole = z_recv[0]
    for z in range(1, 16):
        whole = whole + z_recv[z]
    ag_recv[flat] = whole * (1.0 / math.sqrt(SITES * PLANES))

    for d in FLAT_ORDER:
        if d < 16:
            pltpu.make_async_remote_copy(
                src_ref=ag_recv.at[flat], dst_ref=ag_recv.at[flat], send_sem=ag_sems.at[0],
                recv_sem=ag_sems.at[1], device_id=flat_peer(d), device_id_type=MESH,
            ).start()

    ag_others = ag_recv.at[pl.ds(0, 15)]
    pltpu.make_async_copy(ag_others, ag_others, ag_sems.at[1]).wait()
    for part in range(2):
        for tile in range(8):
            out[part, :, tile * LANES : (tile + 1) * LANES] = ag_recv[part * 8 + tile]

    pltpu.make_async_copy(st_three, st_three, st_sems.at[0]).wait()
    shift.wait_send()
    phi_three = phi_recv.at[:, pl.ds(0, 3)]
    pltpu.make_async_copy(phi_three, phi_three, phi_send_sem.at[0]).wait()
    pltpu.make_async_copy(e_recv, e_recv, e_sems.at[2]).wait()
    pltpu.make_async_copy(z_same, z_same, z_sems.at[2]).wait()
    pltpu.make_async_copy(z_other, z_other, z_sems.at[2]).wait()
    pltpu.make_async_copy(ag_others, ag_others, ag_sems.at[0]).wait()


def shards(vectors, gauge_links, momentum, directions, blocks):
    nblk = vectors.shape[0]
    vec = vectors.transpose(0, 2, 3, 1, 4).reshape(nblk, 48, SITES)
    links = gauge_links.reshape(3, 18, SITES)
    return pl.pallas_call(
        kernel,
        name="elementals",
        out_shape=jax.ShapeDtypeStruct((2, 8, 1024), F32),
        in_specs=[pl.BlockSpec(memory_space=pl.ANY)] * 5,
        out_specs=pl.BlockSpec(memory_space=pltpu.VMEM),
        scratch_shapes=[
            pltpu.SMEM((3,), jnp.int32),
            pltpu.SMEM((2,), jnp.int32),
            pltpu.SMEM((3,), jnp.int32),
            pltpu.VMEM((nblk, 48, SITES), BF16),
            pltpu.VMEM((3, 18, SITES), BF16),
            pltpu.VMEM((4, 96, QUARTER), BF16),
            pltpu.VMEM((4, 96, QUARTER), BF16),
            pltpu.VMEM((4, 96, QUARTER), F32),
            pltpu.VMEM((48, SITES), F32),
            pltpu.VMEM((48, SITES), BF16),
            pltpu.VMEM((48, SITES), BF16),
            pltpu.VMEM((8, SITES), F32),
            pltpu.VMEM((8, SITES), F32),
            pltpu.VMEM((CHUNKS, 4, 48, LANES), BF16),
            pltpu.VMEM((CHUNKS, 4, 48, LANES), BF16),
            pltpu.VMEM((CHUNKS, 1024, 6 * LANES), BF16),
            pltpu.VMEM((2, 2, 16, 8, LANES), F32),
            pltpu.VMEM((2, 31, 8, LANES), F32),
            pltpu.VMEM((2, 8, LANES), F32),
            pltpu.VMEM((16, 8, LANES), F32),
            pltpu.VMEM((16, 8, LANES), F32),
            pltpu.SemaphoreType.DMA((5,)),
            pltpu.SemaphoreType.DMA((2,)),
            pltpu.SemaphoreType.DMA((2,)),
            pltpu.SemaphoreType.DMA((2,)),
            pltpu.SemaphoreType.DMA((1,)),
            pltpu.SemaphoreType.DMA((CHUNKS + 1,)),
            pltpu.SemaphoreType.DMA((3,)),
            pltpu.SemaphoreType.DMA((3,)),
            pltpu.SemaphoreType.DMA((2,)),
            pltpu.SemaphoreType.REGULAR((3,)),
        ],
        compiler_params=pltpu.CompilerParams(
            collective_id=1, has_side_effects=True, vmem_limit_bytes=63 * 2**20
        ),
    )(momentum, directions, blocks, vec, links)


def solution(mesh):
    in_specs = (P(None, "vec", None, "space", None), P(None, None, "space", None), P(), P(), P())
    out_specs = P(None, "vec", None)
    return jax.shard_map(shards, mesh=mesh, in_specs=in_specs, out_specs=out_specs, check_vma=False)
```

time: 80.3 us -> 78.6 us (0.979)
  local copies, waits for them, and re-layouts: 4.96 us -> 1.47 us
  Pallas kernels: 75.2 us -> 76.9 us
    unnamed x11 -> x1, local copies, waits for them, and re-layouts: 4.96 us -> 1.47 us
    pallas_call x1, Pallas kernels: 75.2 us -> 76.9 us  [shards(): pl.pallas_call(kernel, name='elementals', out_shape=jax.ShapeDtypeStruct(...]
where the time goes in v2:
time: 78.6 us; the launch traced here: 78.4 us
  Pallas kernels  76.9 us (98%)
  local copies, waits for them, and re-layouts  1.47 us (2%)
    pallas_call x1, Pallas kernels, shards(): pl.pallas_call(kernel, name='elementals', out_shape=jax.ShapeDtypeStruct(...  76.9 us

profile of v2, /device:TPU:1, one launch (start us, length us, event | category | flops | bytes accessed | tf_op | source)
XLA Modules:
  0.0 78.4 jit_solution(10571267489513111692)
XLA Ops:
  0.0 76.9 %elementals.1 = f32[2,8,1024]{2,1,0:T(8,128)} custom-call(s32[3]{0:T(128)} %momentum_hbm.1, s32[2]{0:T(128)} %directions_hbm.1, s32[3]{0:T(128)} %blocks_hbm.1, bf16[8,48,2048]{2,1,0:T(8,128)(2,1)} %bitcast.4, bf16[3,18,2048]{2,1,0:T(8,128)(2,1)} %bitcast.5), custom_call_target="tpu_custom_call" | custom-call | tf_op jit(solution)/shard_map/elementals/pallas_call | solution.py:342
  76.9 1.5 %copy.7 = f32[2,8,1024]{2,1,0:T(8,128)} copy(f32[2,8,1024]{2,1,0:T(8,128)} %elementals.1) | data formatting | bytes 131072

commit v3 on v2

--- a/solution.py
+++ b/solution.py
@@ -50,7 +50,7 @@
 
 def kernel(
     momentum_hbm, directions_hbm, blocks_hbm, vec_hbm, links_hbm, out,
-    momentum, directions, blocks, vec_v, links_v, st_send, st_recv, st_wide, roll_v, shift_send, shift_recv, cos_v, sin_v,
+    momentum, directions, blocks, vec_v, links_v, st_send, st_recv, st_wide, roll_v, shift_send, shift_recv, piece, piece_low, cos_v, sin_v,
     phi_send, phi_recv, table, e_send, e_recv, z_send, z_recv, ag_recv,
     load_sem, own_sem, shift_sems, st_sems, phi_send_sem, phi_recv_sems, e_sems, z_sems, ag_sems, known_sems,
 ):
@@ -74,8 +74,10 @@
     def vec_peer(d):
         return space, lax.rem(vec + d, 4)
 
-    below = (lax.rem(space + PLANES - 1, PLANES), vec)
-    above = (lax.rem(space + 1, PLANES), vec)
+    layer = zlow * 16
+    up = (lax.rem(zlow + 1, 8) * 16 + flat, vec)
+    down = (lax.rem(zlow + 7, 8) * 16 + flat, vec)
+    last = lax.div(flat, 15)
     near = half * 2 + (1 - core)
     cross_core = (space, (1 - half) * 2 + (1 - core))
 
@@ -88,8 +90,7 @@
     greet(cross_core)
     greet(z_peer(1))
     greet(z_peer(15))
-    greet(below)
-    greet(above)
+    greet(up)
 
     @pl.loop(1, 32)
     def _(d):
@@ -122,18 +123,6 @@
         st_send[q, 0:48] = vec_v[blocks[1], :, at]
         st_send[q, 48:96] = vec_v[blocks[2], :, at]
 
-    pl.semaphore_wait(barrier, 31 + 6)
-
-    for d in (2, 1, 3):
-        target = lax.rem(vec + d, 4)
-        pltpu.make_async_remote_copy(
-            src_ref=st_send.at[target], dst_ref=st_recv.at[vec], send_sem=st_sems.at[0],
-            recv_sem=st_sems.at[1], device_id=vec_peer(d), device_id_type=MESH,
-        ).start()
-    pass_on(0, 1)
-    own_st = pltpu.make_async_copy(st_send.at[vec], st_recv.at[vec], own_sem.at[0])
-    own_st.start()
-
     for b in range(6):
         row = vec_v[blocks[0], (b // 2) * 16 : (b // 2) * 16 + 16, :].astype(F32)
         row = row[(b % 2) * 8 : (b % 2) * 8 + 8]
@@ -146,11 +135,38 @@
         moved = jnp.concatenate(link_rows(links, roll_v[:, at]), axis=0).astype(BF16)
         shift_send[:, at] = jnp.where(z_first, vec_v[blocks[0], :, at], moved)
 
-    shift = pltpu.make_async_remote_copy(
-        src_ref=shift_send, dst_ref=shift_recv, send_sem=shift_sems.at[0], recv_sem=shift_sems.at[1],
-        device_id=below, device_id_type=MESH,
-    )
-    shift.start()
+    pl.semaphore_wait(barrier, 31 + 5)
+
+    @pl.when(flat != 0)
+    def _():
+        pltpu.make_async_remote_copy(
+            src_ref=shift_send, dst_ref=shift_recv, send_sem=shift_sems.at[0], recv_sem=shift_sems.at[1],
+            device_id=(space - 1, vec), device_id_type=MESH,
+        ).start()
+
+    @pl.when(flat == 0)
+    def _():
+        pltpu.make_async_copy(shift_send.at[:, pl.ds(0, LANES)], piece, shift_sems.at[2]).start()
+        for k in range(15, 0, -1):
+            pltpu.make_async_remote_copy(
+                src_ref=shift_send.at[:, pl.ds(k * LANES, LANES)], dst_ref=piece, send_sem=shift_sems.at[0],
+                recv_sem=shift_sems.at[2], device_id=(layer + k, vec), device_id_type=MESH,
+            ).start()
+
+    def exchange(role):
+        rows = pl.ds(role * 48, 48)
+        for d in (2, 1, 3):
+            target = lax.rem(vec + d, 4)
+            pltpu.make_async_remote_copy(
+                src_ref=st_send.at[target, rows], dst_ref=st_recv.at[vec, rows], send_sem=st_sems.at[0],
+                recv_sem=st_sems.at[1], device_id=vec_peer(d), device_id_type=MESH,
+            ).start()
+
+    exchange(0)
+    pass_on(0, 1)
+    own_st = pltpu.make_async_copy(st_send.at[vec], st_recv.at[vec], own_sem.at[0])
+    own_st.start()
+
     pl.semaphore_wait(known_sems.at[0], 2)
     pass_on(1, 2)
     site = lax.broadcasted_iota(jnp.int32, (8, SITES), 1)
@@ -161,46 +177,75 @@
     cos_v[...] = jnp.cos(angles)
     sin_v[...] = jnp.sin(angles)
 
-    shift.wait_recv()
+    pltpu.make_async_copy(piece, piece, shift_sems.at[2]).wait()
+
+    def forward(dst, sem):
+        pltpu.make_async_remote_copy(
+            src_ref=piece, dst_ref=dst, send_sem=shift_sems.at[3], recv_sem=sem, device_id=down, device_id_type=MESH,
+        ).start()
+
+    @pl.when(flat != 15)
+    def _():
+        forward(piece_low, shift_sems.at[4])
+
+    @pl.when(flat == 15)
+    def _():
+        forward(shift_recv.at[:, pl.ds(15 * LANES, LANES)], shift_sems.at[1])
+
+    exchange(1)
     pl.semaphore_wait(known_sems.at[1], 2)
     pass_on(2, 4)
 
-    @pl.loop(0, SITES // 256)
-    def _(t):
-        at = pl.ds(t * 256, 256)
-        links = links_v[2, :, at].astype(F32)
-        moved = jnp.concatenate(link_rows(links, shift_recv[:, at].astype(F32)), axis=0)
-        shift_recv[:, at] = moved.astype(BF16)
-
-    for b in range(6):
-        row = shift_recv[(b // 2) * 16 : (b // 2) * 16 + 16, :].astype(F32)
-        row = row[(b % 2) * 8 : (b % 2) * 8 + 8]
-        roll_v[b * 8 : b * 8 + 8] = rolled(inplane, row)
-
-    @pl.loop(0, SITES // LANES)
-    def _(t):
-        at = pl.ds(t * LANES, LANES)
-        links = links_v[inplane, :, at].astype(F32)
-        moved = jnp.concatenate(link_rows(links, roll_v[:, at]), axis=0).astype(BF16)
-        moved = jnp.where(z_first, moved, shift_recv[:, at]).astype(F32)
-        cosines = cos_v[:, at]
-        sines = sin_v[:, at]
-        rows = []
-        for a in range(3):
-            re = moved[16 * a : 16 * a + 8]
-            im = moved[16 * a + 8 : 16 * a + 16]
-            rows += [cosines * re + sines * im, cosines * im - sines * re]
-        phi_send[lax.rem(t, CHUNKS), lax.div(t, CHUNKS)] = jnp.concatenate(rows, axis=0).astype(BF16)
-
-    for n in range(CHUNKS):
-        for d, sem in ((2, phi_recv_sems.at[n]), (None, phi_recv_sems.at[n]), (1, phi_recv_sems.at[CHUNKS])):
-            to_vec = near if d == 1 else (lax.rem(vec + 2, 4) if d == 2 else cross_core[1])
+    def phase_own():
+        pltpu.make_async_copy(shift_recv, shift_recv, shift_sems.at[1]).wait()
+
+        @pl.loop(0, SITES // 256)
+        def _(t):
+            at = pl.ds(t * 256, 256)
+            links = links_v[2, :, at].astype(F32)
+            moved = jnp.concatenate(link_rows(links, shift_recv[:, at].astype(F32)), axis=0)
+            shift_recv[:, at] = moved.astype(BF16)
+
+        for b in range(6):
+            row = shift_recv[(b // 2) * 16 : (b // 2) * 16 + 16, :].astype(F32)
+            row = row[(b % 2) * 8 : (b % 2) * 8 + 8]
+            roll_v[b * 8 : b * 8 + 8] = rolled(inplane, row)
+
+        @pl.loop(0, SITES // LANES)
+        def _(t):
+            at = pl.ds(t * LANES, LANES)
+            links = links_v[inplane, :, at].astype(F32)
+            moved = jnp.concatenate(link_rows(links, roll_v[:, at]), axis=0).astype(BF16)
+            moved = jnp.where(z_first, moved, shift_recv[:, at]).astype(F32)
+            cosines = cos_v[:, at]
+            sines = sin_v[:, at]
+            rows = []
+            for a in range(3):
+                re = moved[16 * a : 16 * a + 8]
+                im = moved[16 * a + 8 : 16 * a + 16]
+                rows += [cosines * re + sines * im, cosines * im - sines * re]
+            phi_send[lax.rem(t, CHUNKS), lax.div(t, CHUNKS)] = jnp.concatenate(rows, axis=0).astype(BF16)
+
+        for n in range(CHUNKS):
+            for d, sem in ((2, phi_recv_sems.at[n]), (None, phi_recv_sems.at[n]), (1, phi_recv_sems.at[CHUNKS])):
+                to_vec = near if d == 1 else (lax.rem(vec + 2, 4) if d == 2 else cross_core[1])
+                pltpu.make_async_remote_copy(
+                    src_ref=phi_send.at[n, to_vec], dst_ref=phi_recv.at[n, vec], send_sem=phi_send_sem.at[0],
+                    recv_sem=sem, device_id=(space, to_vec), device_id_type=MESH,
+                ).start()
+        pltpu.make_async_copy(phi_send.at[:, vec], phi_recv.at[:, vec], own_sem.at[1]).start()
+
+    @pl.loop(0, 2)
+    def _(turn):
+        pl.when(turn == last)(phase_own)
+
+        @pl.when((turn == 0) & (flat != 15))
+        def _():
+            pltpu.make_async_copy(piece_low, piece_low, shift_sems.at[4]).wait()
             pltpu.make_async_remote_copy(
-                src_ref=phi_send.at[n, to_vec], dst_ref=phi_recv.at[n, vec], send_sem=phi_send_sem.at[0],
-                recv_sem=sem, device_id=(space, to_vec), device_id_type=MESH,
+                src_ref=piece_low, dst_ref=shift_recv.at[:, pl.ds(pl.multiple_of(flat * LANES, LANES), LANES)],
+                send_sem=shift_sems.at[5], recv_sem=shift_sems.at[1], device_id=(layer + 15, vec), device_id_type=MESH,
             ).start()
-    own_phi = pltpu.make_async_copy(phi_send.at[:, vec], phi_recv.at[:, vec], own_sem.at[1])
-    own_phi.start()
 
     pl.semaphore_wait(known_sems.at[2], 2)
     st_three = st_recv.at[pl.ds(0, 3)]
@@ -278,8 +323,8 @@
             recv_sem=z_sems.at[at], device_id=(to_space, to_vec), device_id_type=MESH,
         ).start()
 
-    own_phi.wait()
     phi_near = phi_recv.at[:, 0]
+    pltpu.make_async_copy(phi_near, phi_near, own_sem.at[1]).wait()
     pltpu.make_async_copy(phi_near, phi_near, phi_recv_sems.at[CHUNKS]).wait()
     total = product(0, half)
     for n in range(1, CHUNKS):
@@ -326,7 +371,21 @@
             out[part, :, tile * LANES : (tile + 1) * LANES] = ag_recv[part * 8 + tile]
 
     pltpu.make_async_copy(st_three, st_three, st_sems.at[0]).wait()
-    shift.wait_send()
+    @pl.when(flat != 0)
+    def _():
+        pltpu.make_async_copy(shift_recv, shift_recv, shift_sems.at[0]).wait()
+
+    @pl.when(flat == 0)
+    def _():
+        pieces = shift_recv.at[:, pl.ds(0, 15 * LANES)]
+        pltpu.make_async_copy(pieces, pieces, shift_sems.at[0]).wait()
+
+    pltpu.make_async_copy(piece, piece, shift_sems.at[3]).wait()
+
+    @pl.when(flat != 15)
+    def _():
+        pltpu.make_async_copy(piece_low, piece_low, shift_sems.at[5]).wait()
+
     phi_three = phi_recv.at[:, pl.ds(0, 3)]
     pltpu.make_async_copy(phi_three, phi_three, phi_send_sem.at[0]).wait()
     pltpu.make_async_copy(e_recv, e_recv, e_sems.at[2]).wait()
@@ -357,6 +416,8 @@
             pltpu.VMEM((48, SITES), F32),
             pltpu.VMEM((48, SITES), BF16),
             pltpu.VMEM((48, SITES), BF16),
+            pltpu.VMEM((48, LANES), BF16),
+            pltpu.VMEM((48, LANES), BF16),
             pltpu.VMEM((8, SITES), F32),
             pltpu.VMEM((8, SITES), F32),
             pltpu.VMEM((CHUNKS, 4, 48, LANES), BF16),
@@ -369,7 +430,7 @@
             pltpu.VMEM((16, 8, LANES), F32),
             pltpu.SemaphoreType.DMA((5,)),
             pltpu.SemaphoreType.DMA((2,)),
-            pltpu.SemaphoreType.DMA((2,)),
+            pltpu.SemaphoreType.DMA((6,)),
             pltpu.SemaphoreType.DMA((2,)),
             pltpu.SemaphoreType.DMA((1,)),
             pltpu.SemaphoreType.DMA((CHUNKS + 1,)),

time: 78.6 us -> 71.3 us (0.907)
  Pallas kernels: 76.9 us -> 69.6 us
    pallas_call x1, Pallas kernels: 76.9 us -> 69.6 us  [shards(): pl.pallas_call(kernel, name='elementals', out_shape=jax.ShapeDtypeStruct(...]
where the time goes in v3:
time: 71.3 us; the launch traced here: 71.1 us
  Pallas kernels  69.6 us (98%)
  local copies, waits for them, and re-layouts  1.47 us (2%)
    pallas_call x1, Pallas kernels, shards(): pl.pallas_call(kernel, name='elementals', out_shape=jax.ShapeDtypeStruct(...  69.6 us
    unnamed x1, local copies, waits for them, and re-layouts  1.47 us

profile of v3, /device:TPU:1, one launch (start us, length us, event | category | flops | bytes accessed | tf_op | source)
XLA Modules:
  0.0 71.1 jit_solution(7922723739259245486)
XLA Ops:
  0.0 69.6 %elementals.1 = f32[2,8,1024]{2,1,0:T(8,128)} custom-call(s32[3]{0:T(128)} %momentum_hbm.1, s32[2]{0:T(128)} %directions_hbm.1, s32[3]{0:T(128)} %blocks_hbm.1, bf16[8,48,2048]{2,1,0:T(8,128)(2,1)} %bitcast.4, bf16[3,18,2048]{2,1,0:T(8,128)(2,1)} %bitcast.5), custom_call_target="tpu_custom_call" | custom-call | tf_op jit(solution)/shard_map/elementals/pallas_call | solution.py:401
  69.6 1.5 %copy.7 = f32[2,8,1024]{2,1,0:T(8,128)} copy(f32[2,8,1024]{2,1,0:T(8,128)} %elementals.1) | data formatting | bytes 131072

commit v4 on v3

--- a/solution.py
+++ b/solution.py
@@ -19,6 +19,7 @@
 LANES = 128
 QUARTER = SITES // 4
 CHUNKS = QUARTER // LANES
+HALF = QUARTER // 2
 FLAT_ORDER = sorted(range(1, 32), key=lambda d: -(min(d // 4 % 4, 4 - d // 4 % 4) + min(d % 4, 4 - d % 4)))
 
 
@@ -119,9 +120,10 @@
     inplane = jnp.where(z_first, directions[1], first_step)
 
     for q in range(4):
-        at = slice(q * QUARTER, (q + 1) * QUARTER)
-        st_send[q, 0:48] = vec_v[blocks[1], :, at]
-        st_send[q, 48:96] = vec_v[blocks[2], :, at]
+        for part in range(2):
+            at = slice(q * QUARTER + part * HALF, q * QUARTER + (part + 1) * HALF)
+            st_send[part, q, 0:48] = vec_v[blocks[1], :, at]
+            st_send[part, q, 48:96] = vec_v[blocks[2], :, at]
 
     for b in range(6):
         row = vec_v[blocks[0], (b // 2) * 16 : (b // 2) * 16 + 16, :].astype(F32)
@@ -153,20 +155,17 @@
                 recv_sem=shift_sems.at[2], device_id=(layer + k, vec), device_id_type=MESH,
             ).start()
 
-    def exchange(role):
-        rows = pl.ds(role * 48, 48)
+    def exchange(part):
         for d in (2, 1, 3):
             target = lax.rem(vec + d, 4)
             pltpu.make_async_remote_copy(
-                src_ref=st_send.at[target, rows], dst_ref=st_recv.at[vec, rows], send_sem=st_sems.at[0],
-                recv_sem=st_sems.at[1], device_id=vec_peer(d), device_id_type=MESH,
+                src_ref=st_send.at[part, target], dst_ref=st_recv.at[part, vec], send_sem=st_sems.at[2],
+                recv_sem=st_sems.at[part], device_id=vec_peer(d), device_id_type=MESH,
             ).start()
+        pltpu.make_async_copy(st_send.at[part, vec], st_recv.at[part, vec], own_sem.at[part]).start()
 
     exchange(0)
     pass_on(0, 1)
-    own_st = pltpu.make_async_copy(st_send.at[vec], st_recv.at[vec], own_sem.at[0])
-    own_st.start()
-
     pl.semaphore_wait(known_sems.at[0], 2)
     pass_on(1, 2)
     site = lax.broadcasted_iota(jnp.int32, (8, SITES), 1)
@@ -226,14 +225,11 @@
                 rows += [cosines * re + sines * im, cosines * im - sines * re]
             phi_send[lax.rem(t, CHUNKS), lax.div(t, CHUNKS)] = jnp.concatenate(rows, axis=0).astype(BF16)
 
-        for n in range(CHUNKS):
-            for d, sem in ((2, phi_recv_sems.at[n]), (None, phi_recv_sems.at[n]), (1, phi_recv_sems.at[CHUNKS])):
-                to_vec = near if d == 1 else (lax.rem(vec + 2, 4) if d == 2 else cross_core[1])
-                pltpu.make_async_remote_copy(
-                    src_ref=phi_send.at[n, to_vec], dst_ref=phi_recv.at[n, vec], send_sem=phi_send_sem.at[0],
-                    recv_sem=sem, device_id=(space, to_vec), device_id_type=MESH,
-                ).start()
-        pltpu.make_async_copy(phi_send.at[:, vec], phi_recv.at[:, vec], own_sem.at[1]).start()
+        pltpu.make_async_copy(phi_send.at[:, vec], phi_recv.at[:, vec], own_sem.at[2]).start()
+        pltpu.make_async_remote_copy(
+            src_ref=phi_send.at[:, near], dst_ref=phi_recv.at[:, vec], send_sem=phi_send_sem.at[0],
+            recv_sem=phi_recv_sems.at[CHUNKS], device_id=(space, near), device_id_type=MESH,
+        ).start()
 
     @pl.loop(0, 2)
     def _(turn):
@@ -248,41 +244,52 @@
             ).start()
 
     pl.semaphore_wait(known_sems.at[2], 2)
-    st_three = st_recv.at[pl.ds(0, 3)]
-    own_st.wait()
-    pltpu.make_async_copy(st_three, st_three, st_sems.at[1]).wait()
-
-    @pl.loop(0, 4)
-    def _(source):
-        st_wide[source] = st_recv[source].astype(F32)
-
-    @pl.loop(0, CHUNKS * 4)
-    def _(turn):
-        n = lax.div(turn, 4)
-        source = lax.rem(turn, 4)
-        at = pl.ds(n * LANES, LANES)
-        right = [[st_wide[k, 48 + 8 * b : 56 + 8 * b, at] for b in range(6)] for k in range(4)]
-        for j in range(8):
-            left = [
-                jnp.broadcast_to(st_wide[source, 8 * b + j : 8 * b + j + 1, at], (8, LANES)) for b in range(6)
-            ]
-            start = source * 256 + j * 32
-            for a in range(3):
-                b = 2 * ((a + 1) % 3)
-                c = 2 * ((a + 2) % 3)
-                reals = []
-                imags = []
-                for k in range(4):
-                    rbr, rbi, rcr, rci = right[k][b], right[k][b + 1], right[k][c], right[k][c + 1]
-                    lbr, lbi, lcr, lci = left[b], left[b + 1], left[c], left[c + 1]
-                    reals.append(lbr * rcr - lbi * rci - (lcr * rbr - lci * rbi))
-                    imags.append(lbr * rci + lbi * rcr - (lcr * rbi + lci * rbr))
-                table[n, pl.ds(start, 32), 2 * a * LANES : (2 * a + 1) * LANES] = jnp.concatenate(
-                    reals, axis=0
-                ).astype(BF16)
-                table[n, pl.ds(start, 32), (2 * a + 1) * LANES : (2 * a + 2) * LANES] = jnp.concatenate(
-                    imags, axis=0
-                ).astype(BF16)
+    def send_far():
+        for n in range(CHUNKS):
+            for to_vec in (lax.rem(vec + 2, 4), cross_core[1]):
+                pltpu.make_async_remote_copy(
+                    src_ref=phi_send.at[n, to_vec], dst_ref=phi_recv.at[n, vec], send_sem=phi_send_sem.at[0],
+                    recv_sem=phi_recv_sems.at[n], device_id=(space, to_vec), device_id_type=MESH,
+                ).start()
+
+    st_three = st_recv.at[0, pl.ds(0, 3)]
+
+    def make_table(part):
+        own_st = st_recv.at[part, 0]
+        pltpu.make_async_copy(own_st, own_st, own_sem.at[part]).wait()
+        pltpu.make_async_copy(st_three, st_three, st_sems.at[part]).wait()
+
+        @pl.loop(0, 4)
+        def _(source):
+            st_wide[source] = st_recv[part, source].astype(F32)
+
+        @pl.loop(0, 8)
+        def _(turn):
+            n = part * 2 + lax.div(turn, 4)
+            source = lax.rem(turn, 4)
+            at = pl.ds(lax.div(turn, 4) * LANES, LANES)
+            right = [[st_wide[k, 48 + 8 * b : 56 + 8 * b, at] for b in range(6)] for k in range(4)]
+            for j in range(8):
+                left = [
+                    jnp.broadcast_to(st_wide[source, 8 * b + j : 8 * b + j + 1, at], (8, LANES)) for b in range(6)
+                ]
+                start = source * 256 + j * 32
+                for a in range(3):
+                    b = 2 * ((a + 1) % 3)
+                    c = 2 * ((a + 2) % 3)
+                    reals = []
+                    imags = []
+                    for k in range(4):
+                        rbr, rbi, rcr, rci = right[k][b], right[k][b + 1], right[k][c], right[k][c + 1]
+                        lbr, lbi, lcr, lci = left[b], left[b + 1], left[c], left[c + 1]
+                        reals.append(lbr * rcr - lbi * rci - (lcr * rbr - lci * rbi))
+                        imags.append(lbr * rci + lbi * rcr - (lcr * rbi + lci * rbr))
+                    table[n, pl.ds(start, 32), 2 * a * LANES : (2 * a + 1) * LANES] = jnp.concatenate(
+                        reals, axis=0
+                    ).astype(BF16)
+                    table[n, pl.ds(start, 32), (2 * a + 1) * LANES : (2 * a + 2) * LANES] = jnp.concatenate(
+                        imags, axis=0
+                    ).astype(BF16)
 
     def product(n, whose):
         real_rows = []
@@ -323,12 +330,16 @@
             recv_sem=z_sems.at[at], device_id=(to_space, to_vec), device_id_type=MESH,
         ).start()
 
+    make_table(0)
     phi_near = phi_recv.at[:, 0]
-    pltpu.make_async_copy(phi_near, phi_near, own_sem.at[1]).wait()
+    pltpu.make_async_copy(phi_near, phi_near, own_sem.at[2]).wait()
     pltpu.make_async_copy(phi_near, phi_near, phi_recv_sems.at[CHUNKS]).wait()
-    total = product(0, half)
-    for n in range(1, CHUNKS):
-        total = total + product(n, half)
+    total = product(0, half) + product(1, half)
+    for part in range(2):
+        pltpu.make_async_copy(st_three, st_three, st_sems.at[2]).wait()
+    send_far()
+    make_table(1)
+    total = total + product(2, half) + product(3, half)
     scatter(0, total)
 
     total = None
@@ -370,7 +381,6 @@
         for tile in range(8):
             out[part, :, tile * LANES : (tile + 1) * LANES] = ag_recv[part * 8 + tile]
 
-    pltpu.make_async_copy(st_three, st_three, st_sems.at[0]).wait()
     @pl.when(flat != 0)
     def _():
         pltpu.make_async_copy(shift_recv, shift_recv, shift_sems.at[0]).wait()
@@ -410,9 +420,9 @@
             pltpu.SMEM((3,), jnp.int32),
             pltpu.VMEM((nblk, 48, SITES), BF16),
             pltpu.VMEM((3, 18, SITES), BF16),
-            pltpu.VMEM((4, 96, QUARTER), BF16),
-            pltpu.VMEM((4, 96, QUARTER), BF16),
-            pltpu.VMEM((4, 96, QUARTER), F32),
+            pltpu.VMEM((2, 4, 96, HALF), BF16),
+            pltpu.VMEM((2, 4, 96, HALF), BF16),
+            pltpu.VMEM((4, 96, HALF), F32),
             pltpu.VMEM((48, SITES), F32),
             pltpu.VMEM((48, SITES), BF16),
             pltpu.VMEM((48, SITES), BF16),
@@ -429,9 +439,9 @@
             pltpu.VMEM((16, 8, LANES), F32),
             pltpu.VMEM((16, 8, LANES), F32),
             pltpu.SemaphoreType.DMA((5,)),
-            pltpu.SemaphoreType.DMA((2,)),
+            pltpu.SemaphoreType.DMA((3,)),
             pltpu.SemaphoreType.DMA((6,)),
-            pltpu.SemaphoreType.DMA((2,)),
+            pltpu.SemaphoreType.DMA((3,)),
             pltpu.SemaphoreType.DMA((1,)),
             pltpu.SemaphoreType.DMA((CHUNKS + 1,)),
             pltpu.SemaphoreType.DMA((3,)),

time: 71.3 us -> 68.6 us (0.962)
  Pallas kernels: 69.6 us -> 66.9 us
    pallas_call x1, Pallas kernels: 69.6 us -> 66.9 us  [shards(): pl.pallas_call(kernel, name='elementals', out_shape=jax.ShapeDtypeStruct(...]
where the time goes in v4:
time: 68.6 us; the launch traced here: 68.4 us
  Pallas kernels  66.9 us (98%)
  local copies, waits for them, and re-layouts  1.47 us (2%)
    pallas_call x1, Pallas kernels, shards(): pl.pallas_call(kernel, name='elementals', out_shape=jax.ShapeDtypeStruct(...  66.9 us
    unnamed x1, local copies, waits for them, and re-layouts  1.47 us

profile of v4, /device:TPU:1, one launch (start us, length us, event | category | flops | bytes accessed | tf_op | source)
XLA Modules:
  0.0 68.4 jit_solution(16876461409270419985)
XLA Ops:
  0.0 66.9 %elementals.1 = f32[2,8,1024]{2,1,0:T(8,128)} custom-call(s32[3]{0:T(128)} %momentum_hbm.1, s32[2]{0:T(128)} %directions_hbm.1, s32[3]{0:T(128)} %blocks_hbm.1, bf16[8,48,2048]{2,1,0:T(8,128)(2,1)} %bitcast.4, bf16[3,18,2048]{2,1,0:T(8,128)(2,1)} %bitcast.5), custom_call_target="tpu_custom_call" | custom-call | tf_op jit(solution)/shard_map/elementals/pallas_call | solution.py:411
  67.0 1.5 %copy.7 = f32[2,8,1024]{2,1,0:T(8,128)} copy(f32[2,8,1024]{2,1,0:T(8,128)} %elementals.1) | data formatting | bytes 131072

commit v5 on v4

--- a/solution.py
+++ b/solution.py
@@ -52,7 +52,7 @@
 def kernel(
     momentum_hbm, directions_hbm, blocks_hbm, vec_hbm, links_hbm, out,
     momentum, directions, blocks, vec_v, links_v, st_send, st_recv, st_wide, roll_v, shift_send, shift_recv, piece, piece_low, cos_v, sin_v,
-    phi_send, phi_recv, table, e_send, e_recv, z_send, z_recv, ag_recv,
+    phi_send, phi_recv, table, e_send, e_recv, z_send, z_recv, mine,
     load_sem, own_sem, shift_sems, st_sems, phi_send_sem, phi_recv_sems, e_sems, z_sems, ag_sems, known_sems,
 ):
     space = lax.axis_index("space")
@@ -155,16 +155,17 @@
                 recv_sem=shift_sems.at[2], device_id=(layer + k, vec), device_id_type=MESH,
             ).start()
 
-    def exchange(part):
-        for d in (2, 1, 3):
+    def exchange(part, steps):
+        for d in steps:
             target = lax.rem(vec + d, 4)
             pltpu.make_async_remote_copy(
                 src_ref=st_send.at[part, target], dst_ref=st_recv.at[part, vec], send_sem=st_sems.at[2],
                 recv_sem=st_sems.at[part], device_id=vec_peer(d), device_id_type=MESH,
             ).start()
+
+    exchange(0, (2, 1))
+    for part in range(2):
         pltpu.make_async_copy(st_send.at[part, vec], st_recv.at[part, vec], own_sem.at[part]).start()
-
-    exchange(0)
     pass_on(0, 1)
     pl.semaphore_wait(known_sems.at[0], 2)
     pass_on(1, 2)
@@ -191,7 +192,8 @@
     def _():
         forward(shift_recv.at[:, pl.ds(15 * LANES, LANES)], shift_sems.at[1])
 
-    exchange(1)
+    exchange(0, (3,))
+    exchange(1, (2, 3, 1))
     pl.semaphore_wait(known_sems.at[1], 2)
     pass_on(2, 4)
 
@@ -366,20 +368,17 @@
     whole = z_recv[0]
     for z in range(1, 16):
         whole = whole + z_recv[z]
-    ag_recv[flat] = whole * (1.0 / math.sqrt(SITES * PLANES))
+    mine[...] = whole * (1.0 / math.sqrt(SITES * PLANES))
+    place = out.at[lax.div(flat, 8), :, pl.ds(pl.multiple_of(lax.rem(flat, 8) * LANES, LANES), LANES)]
+    own_out = pltpu.make_async_copy(mine, place, load_sem.at[0])
+    own_out.start()
 
     for d in FLAT_ORDER:
         if d < 16:
             pltpu.make_async_remote_copy(
-                src_ref=ag_recv.at[flat], dst_ref=ag_recv.at[flat], send_sem=ag_sems.at[0],
+                src_ref=mine, dst_ref=place, send_sem=ag_sems.at[0],
                 recv_sem=ag_sems.at[1], device_id=flat_peer(d), device_id_type=MESH,
             ).start()
-
-    ag_others = ag_recv.at[pl.ds(0, 15)]
-    pltpu.make_async_copy(ag_others, ag_others, ag_sems.at[1]).wait()
-    for part in range(2):
-        for tile in range(8):
-            out[part, :, tile * LANES : (tile + 1) * LANES] = ag_recv[part * 8 + tile]
 
     @pl.when(flat != 0)
     def _():
@@ -401,7 +400,10 @@
     pltpu.make_async_copy(e_recv, e_recv, e_sems.at[2]).wait()
     pltpu.make_async_copy(z_same, z_same, z_sems.at[2]).wait()
     pltpu.make_async_copy(z_other, z_other, z_sems.at[2]).wait()
+    own_out.wait()
+    ag_others = z_recv.at[pl.ds(0, 15)]
     pltpu.make_async_copy(ag_others, ag_others, ag_sems.at[0]).wait()
+    pltpu.make_async_copy(ag_others, ag_others, ag_sems.at[1]).wait()
 
 
 def shards(vectors, gauge_links, momentum, directions, blocks):
@@ -413,7 +415,7 @@
         name="elementals",
         out_shape=jax.ShapeDtypeStruct((2, 8, 1024), F32),
         in_specs=[pl.BlockSpec(memory_space=pl.ANY)] * 5,
-        out_specs=pl.BlockSpec(memory_space=pltpu.VMEM),
+        out_specs=pl.BlockSpec(memory_space=pl.ANY),
         scratch_shapes=[
             pltpu.SMEM((3,), jnp.int32),
             pltpu.SMEM((2,), jnp.int32),
@@ -437,7 +439,7 @@
             pltpu.VMEM((2, 31, 8, LANES), F32),
             pltpu.VMEM((2, 8, LANES), F32),
             pltpu.VMEM((16, 8, LANES), F32),
-            pltpu.VMEM((16, 8, LANES), F32),
+            pltpu.VMEM((8, LANES), F32),
             pltpu.SemaphoreType.DMA((5,)),
             pltpu.SemaphoreType.DMA((3,)),
             pltpu.SemaphoreType.DMA((6,)),

time: 68.6 us -> 67.2 us (0.980)
  Pallas kernels: 66.9 us -> 65.6 us
    pallas_call x1, Pallas kernels: 66.9 us -> 65.6 us  [shards(): pl.pallas_call(kernel, name='elementals', out_shape=jax.ShapeDtypeStruct(...]
where the time goes in v5:
time: 67.2 us; the launch traced here: 67 us
  Pallas kernels  65.6 us (98%)
  local copies, waits for them, and re-layouts  1.47 us (2%)
    pallas_call x1, Pallas kernels, shards(): pl.pallas_call(kernel, name='elementals', out_shape=jax.ShapeDtypeStruct(...  65.6 us
    unnamed x1, local copies, waits for them, and re-layouts  1.47 us

profile of v5, /device:TPU:1, one launch (start us, length us, event | category | flops | bytes accessed | tf_op | source)
XLA Modules:
  0.0 67.0 jit_solution(11891377967107562124)
XLA Ops:
  0.0 65.6 %elementals.1 = f32[2,8,1024]{2,1,0:T(8,128)} custom-call(s32[3]{0:T(128)} %momentum_hbm.1, s32[2]{0:T(128)} %directions_hbm.1, s32[3]{0:T(128)} %blocks_hbm.1, bf16[8,48,2048]{2,1,0:T(8,128)(2,1)} %bitcast.4, bf16[3,18,2048]{2,1,0:T(8,128)(2,1)} %bitcast.5), custom_call_target="tpu_custom_call" | custom-call | tf_op jit(solution)/shard_map/elementals/pallas_call | solution.py:413
  65.6 1.5 %copy.7 = f32[2,8,1024]{2,1,0:T(8,128)} copy(f32[2,8,1024]{2,1,0:T(8,128)} %elementals.1) | data formatting | bytes 131072

commit v6 on v5

--- a/solution.py
+++ b/solution.py
@@ -19,7 +19,6 @@
 LANES = 128
 QUARTER = SITES // 4
 CHUNKS = QUARTER // LANES
-HALF = QUARTER // 2
 FLAT_ORDER = sorted(range(1, 32), key=lambda d: -(min(d // 4 % 4, 4 - d // 4 % 4) + min(d % 4, 4 - d % 4)))
 
 
@@ -101,8 +100,8 @@
         pltpu.make_async_copy(source, target, load_sem.at[at])
         for at, (source, target) in enumerate(
             (
-                (blocks_hbm, blocks), (vec_hbm, vec_v), (links_hbm, links_v),
-                (directions_hbm, directions), (momentum_hbm, momentum),
+                (blocks_hbm, blocks), (directions_hbm, directions), (momentum_hbm, momentum), (links_hbm, links_v),
+                *((vec_hbm.at[k], vec_v.at[k]) for k in range(vec_v.shape[0])),
             )
         )
     ]
@@ -120,8 +119,8 @@
     inplane = jnp.where(z_first, directions[1], first_step)
 
     for q in range(4):
-        for part in range(2):
-            at = slice(q * QUARTER + part * HALF, q * QUARTER + (part + 1) * HALF)
+        for part in range(CHUNKS):
+            at = slice(q * QUARTER + part * LANES, q * QUARTER + (part + 1) * LANES)
             st_send[part, q, 0:48] = vec_v[blocks[1], :, at]
             st_send[part, q, 48:96] = vec_v[blocks[2], :, at]
 
@@ -159,12 +158,13 @@
         for d in steps:
             target = lax.rem(vec + d, 4)
             pltpu.make_async_remote_copy(
-                src_ref=st_send.at[part, target], dst_ref=st_recv.at[part, vec], send_sem=st_sems.at[2],
+                src_ref=st_send.at[part, target], dst_ref=st_recv.at[part, vec], send_sem=st_sems.at[CHUNKS],
                 recv_sem=st_sems.at[part], device_id=vec_peer(d), device_id_type=MESH,
             ).start()
 
     exchange(0, (2, 1))
-    for part in range(2):
+    exchange(1, (2, 1))
+    for part in range(CHUNKS):
         pltpu.make_async_copy(st_send.at[part, vec], st_recv.at[part, vec], own_sem.at[part]).start()
     pass_on(0, 1)
     pl.semaphore_wait(known_sems.at[0], 2)
@@ -193,7 +193,9 @@
         forward(shift_recv.at[:, pl.ds(15 * LANES, LANES)], shift_sems.at[1])
 
     exchange(0, (3,))
-    exchange(1, (2, 3, 1))
+    exchange(1, (3,))
+    exchange(2, (2, 3, 1))
+    exchange(3, (2, 3, 1))
     pl.semaphore_wait(known_sems.at[1], 2)
     pass_on(2, 4)
 
@@ -227,7 +229,7 @@
                 rows += [cosines * re + sines * im, cosines * im - sines * re]
             phi_send[lax.rem(t, CHUNKS), lax.div(t, CHUNKS)] = jnp.concatenate(rows, axis=0).astype(BF16)
 
-        pltpu.make_async_copy(phi_send.at[:, vec], phi_recv.at[:, vec], own_sem.at[2]).start()
+        pltpu.make_async_copy(phi_send.at[:, vec], phi_recv.at[:, vec], own_sem.at[CHUNKS]).start()
         pltpu.make_async_remote_copy(
             src_ref=phi_send.at[:, near], dst_ref=phi_recv.at[:, vec], send_sem=phi_send_sem.at[0],
             recv_sem=phi_recv_sems.at[CHUNKS], device_id=(space, near), device_id_type=MESH,
@@ -248,7 +250,7 @@
     pl.semaphore_wait(known_sems.at[2], 2)
     def send_far():
         for n in range(CHUNKS):
-            for to_vec in (lax.rem(vec + 2, 4), cross_core[1]):
+            for to_vec in (cross_core[1], lax.rem(vec + 2, 4)):
                 pltpu.make_async_remote_copy(
                     src_ref=phi_send.at[n, to_vec], dst_ref=phi_recv.at[n, vec], send_sem=phi_send_sem.at[0],
                     recv_sem=phi_recv_sems.at[n], device_id=(space, to_vec), device_id_type=MESH,
@@ -265,15 +267,12 @@
         def _(source):
             st_wide[source] = st_recv[part, source].astype(F32)
 
-        @pl.loop(0, 8)
-        def _(turn):
-            n = part * 2 + lax.div(turn, 4)
-            source = lax.rem(turn, 4)
-            at = pl.ds(lax.div(turn, 4) * LANES, LANES)
-            right = [[st_wide[k, 48 + 8 * b : 56 + 8 * b, at] for b in range(6)] for k in range(4)]
+        @pl.loop(0, 4)
+        def _(source):
+            right = [[st_wide[k, 48 + 8 * b : 56 + 8 * b] for b in range(6)] for k in range(4)]
             for j in range(8):
                 left = [
-                    jnp.broadcast_to(st_wide[source, 8 * b + j : 8 * b + j + 1, at], (8, LANES)) for b in range(6)
+                    jnp.broadcast_to(st_wide[source, 8 * b + j : 8 * b + j + 1], (8, LANES)) for b in range(6)
                 ]
                 start = source * 256 + j * 32
                 for a in range(3):
@@ -286,10 +285,10 @@
                         lbr, lbi, lcr, lci = left[b], left[b + 1], left[c], left[c + 1]
                         reals.append(lbr * rcr - lbi * rci - (lcr * rbr - lci * rbi))
                         imags.append(lbr * rci + lbi * rcr - (lcr * rbi + lci * rbr))
-                    table[n, pl.ds(start, 32), 2 * a * LANES : (2 * a + 1) * LANES] = jnp.concatenate(
+                    table[part, pl.ds(start, 32), 2 * a * LANES : (2 * a + 1) * LANES] = jnp.concatenate(
                         reals, axis=0
                     ).astype(BF16)
-                    table[n, pl.ds(start, 32), (2 * a + 1) * LANES : (2 * a + 2) * LANES] = jnp.concatenate(
+                    table[part, pl.ds(start, 32), (2 * a + 1) * LANES : (2 * a + 2) * LANES] = jnp.concatenate(
                         imags, axis=0
                     ).astype(BF16)
 
@@ -333,15 +332,17 @@
         ).start()
 
     make_table(0)
+    make_table(1)
+    for part in range(CHUNKS):
+        pltpu.make_async_copy(st_three, st_three, st_sems.at[CHUNKS]).wait()
+    send_far()
     phi_near = phi_recv.at[:, 0]
-    pltpu.make_async_copy(phi_near, phi_near, own_sem.at[2]).wait()
+    pltpu.make_async_copy(phi_near, phi_near, own_sem.at[CHUNKS]).wait()
     pltpu.make_async_copy(phi_near, phi_near, phi_recv_sems.at[CHUNKS]).wait()
     total = product(0, half) + product(1, half)
-    for part in range(2):
-        pltpu.make_async_copy(st_three, st_three, st_sems.at[2]).wait()
-    send_far()
-    make_table(1)
-    total = total + product(2, half) + product(3, half)
+    for n in (2, 3):
+        make_table(n)
+        total = total + product(n, half)
     scatter(0, total)
 
     total = None
@@ -360,6 +361,25 @@
     z_send[1] = gathered(1)
     for step in (0, 1, 7, 2, 6, 3, 5, 4):
         send_z(1, (1 - half) * 8 + lax.rem(zlow + step, 8) - zee + 16)
+
+    @pl.when(flat != 0)
+    def _():
+        pltpu.make_async_copy(shift_recv, shift_recv, shift_sems.at[0]).wait()
+
+    @pl.when(flat == 0)
+    def _():
+        pieces = shift_recv.at[:, pl.ds(0, 15 * LANES)]
+        pltpu.make_async_copy(pieces, pieces, shift_sems.at[0]).wait()
+
+    pltpu.make_async_copy(piece, piece, shift_sems.at[3]).wait()
+
+    @pl.when(flat != 15)
+    def _():
+        pltpu.make_async_copy(piece_low, piece_low, shift_sems.at[5]).wait()
+
+    phi_three = phi_recv.at[:, pl.ds(0, 3)]
+    pltpu.make_async_copy(phi_three, phi_three, phi_send_sem.at[0]).wait()
+    pltpu.make_async_copy(e_recv, e_recv, e_sems.at[2]).wait()
 
     z_same = z_recv.at[pl.ds(0, 7)]
     z_other = z_recv.at[pl.ds(0, 8)]
@@ -380,24 +400,6 @@
                 recv_sem=ag_sems.at[1], device_id=flat_peer(d), device_id_type=MESH,
             ).start()
 
-    @pl.when(flat != 0)
-    def _():
-        pltpu.make_async_copy(shift_recv, shift_recv, shift_sems.at[0]).wait()
-
-    @pl.when(flat == 0)
-    def _():
-        pieces = shift_recv.at[:, pl.ds(0, 15 * LANES)]
-        pltpu.make_async_copy(pieces, pieces, shift_sems.at[0]).wait()
-
-    pltpu.make_async_copy(piece, piece, shift_sems.at[3]).wait()
-
-    @pl.when(flat != 15)
-    def _():
-        pltpu.make_async_copy(piece_low, piece_low, shift_sems.at[5]).wait()
-
-    phi_three = phi_recv.at[:, pl.ds(0, 3)]
-    pltpu.make_async_copy(phi_three, phi_three, phi_send_sem.at[0]).wait()
-    pltpu.make_async_copy(e_recv, e_recv, e_sems.at[2]).wait()
     pltpu.make_async_copy(z_same, z_same, z_sems.at[2]).wait()
     pltpu.make_async_copy(z_other, z_other, z_sems.at[2]).wait()
     own_out.wait()
@@ -422,9 +424,9 @@
             pltpu.SMEM((3,), jnp.int32),
             pltpu.VMEM((nblk, 48, SITES), BF16),
             pltpu.VMEM((3, 18, SITES), BF16),
-            pltpu.VMEM((2, 4, 96, HALF), BF16),
-            pltpu.VMEM((2, 4, 96, HALF), BF16),
-            pltpu.VMEM((4, 96, HALF), F32),
+            pltpu.VMEM((CHUNKS, 4, 96, LANES), BF16),
+            pltpu.VMEM((CHUNKS, 4, 96, LANES), BF16),
+            pltpu.VMEM((4, 96, LANES), F32),
             pltpu.VMEM((48, SITES), F32),
             pltpu.VMEM((48, SITES), BF16),
             pltpu.VMEM((48, SITES), BF16),
@@ -440,10 +442,10 @@
             pltpu.VMEM((2, 8, LANES), F32),
             pltpu.VMEM((16, 8, LANES), F32),
             pltpu.VMEM((8, LANES), F32),
-            pltpu.SemaphoreType.DMA((5,)),
-            pltpu.SemaphoreType.DMA((3,)),
+            pltpu.SemaphoreType.DMA((4 + nblk,)),
+            pltpu.SemaphoreType.DMA((CHUNKS + 1,)),
             pltpu.SemaphoreType.DMA((6,)),
-            pltpu.SemaphoreType.DMA((3,)),
+            pltpu.SemaphoreType.DMA((CHUNKS + 1,)),
             pltpu.SemaphoreType.DMA((1,)),
             pltpu.SemaphoreType.DMA((CHUNKS + 1,)),
             pltpu.SemaphoreType.DMA((3,)),

time: 67.2 us -> 66.7 us (level)
  no operation moved by 1% of the time
where the time goes in v6:
time: 66.7 us; the launch traced here: 66.5 us
  Pallas kernels  65 us (97%)
  local copies, waits for them, and re-layouts  1.47 us (2%)
    pallas_call x1, Pallas kernels, shards(): pl.pallas_call(kernel, name='elementals', out_shape=jax.ShapeDtypeStruct(...  65 us
    unnamed x1, local copies, waits for them, and re-layouts  1.47 us

profile of v6, /device:TPU:1, one launch (start us, length us, event | category | flops | bytes accessed | tf_op | source)
XLA Modules:
  0.0 66.5 jit_solution(11857798678890984046)
XLA Ops:
  0.0 65.0 %elementals.1 = f32[2,8,1024]{2,1,0:T(8,128)} custom-call(s32[3]{0:T(128)} %momentum_hbm.1, s32[2]{0:T(128)} %directions_hbm.1, s32[3]{0:T(128)} %blocks_hbm.1, bf16[8,48,2048]{2,1,0:T(8,128)(2,1)} %bitcast.4, bf16[3,18,2048]{2,1,0:T(8,128)(2,1)} %bitcast.5), custom_call_target="tpu_custom_call" | custom-call | tf_op jit(solution)/shard_map/elementals/pallas_call | solution.py:415
  65.0 1.5 %copy.7 = f32[2,8,1024]{2,1,0:T(8,128)} copy(f32[2,8,1024]{2,1,0:T(8,128)} %elementals.1) | data formatting | bytes 131072

commit v7 on v6

--- a/solution.py
+++ b/solution.py
@@ -331,11 +331,15 @@
             recv_sem=z_sems.at[at], device_id=(to_space, to_vec), device_id_type=MESH,
         ).start()
 
+    def send_late():
+        for part in range(CHUNKS):
+            pltpu.make_async_copy(st_three, st_three, st_sems.at[CHUNKS]).wait()
+        send_far()
+
+    pl.when(flat == 15)(send_late)
     make_table(0)
     make_table(1)
-    for part in range(CHUNKS):
-        pltpu.make_async_copy(st_three, st_three, st_sems.at[CHUNKS]).wait()
-    send_far()
+    pl.when(flat != 15)(send_late)
     phi_near = phi_recv.at[:, 0]
     pltpu.make_async_copy(phi_near, phi_near, own_sem.at[CHUNKS]).wait()
     pltpu.make_async_copy(phi_near, phi_near, phi_recv_sems.at[CHUNKS]).wait()

time: 66.7 us -> 66.8 us (level)
  no operation moved by 1% of the time
where the time goes in v7:
time: 66.8 us; the launch traced here: 66.6 us
  Pallas kernels  65.1 us (97%)
  local copies, waits for them, and re-layouts  1.47 us (2%)
    pallas_call x1, Pallas kernels, shards(): pl.pallas_call(kernel, name='elementals', out_shape=jax.ShapeDtypeStruct(...  65.1 us
    unnamed x1, local copies, waits for them, and re-layouts  1.47 us

profile of v7, /device:TPU:1, one launch (start us, length us, event | category | flops | bytes accessed | tf_op | source)
XLA Modules:
  0.0 66.6 jit_solution(9295242575967731692)
XLA Ops:
  0.0 65.1 %elementals.1 = f32[2,8,1024]{2,1,0:T(8,128)} custom-call(s32[3]{0:T(128)} %momentum_hbm.1, s32[2]{0:T(128)} %directions_hbm.1, s32[3]{0:T(128)} %blocks_hbm.1, bf16[8,48,2048]{2,1,0:T(8,128)(2,1)} %bitcast.4, bf16[3,18,2048]{2,1,0:T(8,128)(2,1)} %bitcast.5), custom_call_target="tpu_custom_call" | custom-call | tf_op jit(solution)/shard_map/elementals/pallas_call | solution.py:419
  65.1 1.5 %copy.7 = f32[2,8,1024]{2,1,0:T(8,128)} copy(f32[2,8,1024]{2,1,0:T(8,128)} %elementals.1) | data formatting | bytes 131072

commit v8 on v6

--- a/solution.py
+++ b/solution.py
@@ -353,14 +353,14 @@
         total = term if total is None else total + term
     scatter(1, total)
 
+    z_send[1] = gathered(1)
+    for step in (0, 1, 7, 2, 6, 3, 5, 4):
+        send_z(1, (1 - half) * 8 + lax.rem(zlow + step, 8) - zee + 16)
+
     z_send[0] = gathered(0)
     z_recv[zee] = z_send[0]
     for step in range(1, 8):
         send_z(0, half * 8 + lax.rem(zlow + step, 8) - zee + 16)
-
-    z_send[1] = gathered(1)
-    for step in (0, 1, 7, 2, 6, 3, 5, 4):
-        send_z(1, (1 - half) * 8 + lax.rem(zlow + step, 8) - zee + 16)
 
     @pl.when(flat != 0)
     def _():

time: 66.7 us -> 67.9 us (1.018)
  Pallas kernels: 65 us -> 66.2 us
    pallas_call x1, Pallas kernels: 65 us -> 66.2 us  [shards(): pl.pallas_call(kernel, name='elementals', out_shape=jax.ShapeDtypeStruct(...]
where the time goes in v8:
time: 67.9 us; the launch traced here: 67.7 us
  Pallas kernels  66.2 us (97%)
  local copies, waits for them, and re-layouts  1.47 us (2%)
    pallas_call x1, Pallas kernels, shards(): pl.pallas_call(kernel, name='elementals', out_shape=jax.ShapeDtypeStruct(...  66.2 us
    unnamed x1, local copies, waits for them, and re-layouts  1.47 us

profile of v8, /device:TPU:1, one launch (start us, length us, event | category | flops | bytes accessed | tf_op | source)
XLA Modules:
  0.0 67.7 jit_solution(10705128145627315961)
XLA Ops:
  0.0 66.2 %elementals.1 = f32[2,8,1024]{2,1,0:T(8,128)} custom-call(s32[3]{0:T(128)} %momentum_hbm.1, s32[2]{0:T(128)} %directions_hbm.1, s32[3]{0:T(128)} %blocks_hbm.1, bf16[8,48,2048]{2,1,0:T(8,128)(2,1)} %bitcast.4, bf16[3,18,2048]{2,1,0:T(8,128)(2,1)} %bitcast.5), custom_call_target="tpu_custom_call" | custom-call | tf_op jit(solution)/shard_map/elementals/pallas_call | solution.py:415
  66.2 1.5 %copy.7 = f32[2,8,1024]{2,1,0:T(8,128)} copy(f32[2,8,1024]{2,1,0:T(8,128)} %elementals.1) | data formatting | bytes 131072
